TPU v7x, 128 devices: a whole 4x4x4 slice. The times are simulated.
128 devices in a mesh: blk: 32 (over y, x_lo, z), grp: 4 (over x_hi, core).
Axes of the slice: x: 4 (x_hi: 2, x_lo: 2; x = x_hi * 2 + x_lo), y: 4, z: 4, core: 2. Of those that a mesh axis runs over, the one named last changes fastest.
Arguments:
- item_factors: bfloat16 [16384, 256], P('blk'), may hold values from -0.046875 to 0.046875
- exposure: bfloat16 [16384], P('blk'), may hold values from 0.05 to 0.9
- confidence: bfloat16 [128, 128, 128, 128], P(('blk', 'grp')), as said below
- tile_items: int32 [128, 128], P(('blk', 'grp')), may hold values from 0 to 127, as said below
- tile_users: int32 [128, 128], P(('blk', 'grp')), may hold values from 0 to 3, as said below
- tile_count: int32 [128], P(('blk', 'grp')), may hold values from 42 to 128, as said below
Outputs:
- user_factors: bfloat16 [65536, 256], P(('blk', 'grp'))
- item_update: bfloat16 [16384, 256], P(('blk', 'grp'))
- user_gram: float32 [256, 256], replicated
Inputs may be any that keep to these rules, and one draw needn't show every extreme that they name: `tile_items`: row d names an item block for each of device d's 128 tiles, each of the 128 item blocks once; some item block is among the live tiles of every device. `tile_users`: every one of a device's 4 user blocks appears among its first 4 tiles. A device's live tiles are its first tile_count ones; some device has all 128 live. `confidence`: zero where the user has not seen the item, else 1 or more; in every tile each user row and each item column has an entry of 1 or more.
All inputs are finite; a program needn't handle non-finite values.
Results may differ from a plain program's by a relative error of at most 0.0055.
The roundings to bfloat16 on the way count: a program that leaves them out, or rounds other values in their place, can miss the bound.
Values may be sent and summed in bfloat16 or wider, within the bound.
No kernel may reach another device: no remote copies, remote signals or barrier semaphores. Data moves between devices by JAX's collectives and lax.ppermute only.
A program may use at most 192 MiB of HBM per device.

v0:
```python
import jax
import jax.numpy as jnp
from jax import lax
from jax.sharding import PartitionSpec as P

UB_DEV = 4
CG_STEPS = 3


LAMBDA = 1.0
FULL_PRECISION = lax.Precision.HIGHEST


def weighted_gram(factors, weights):
    factor_wide = factors.astype(jnp.float32)
    scaled = factor_wide * weights.astype(jnp.float32)[:, None]
    return lax.dot_general(scaled, factor_wide, (((0,), (0,)), ((), ())), precision=FULL_PRECISION)


def conjugate(right_side, operator, step_count):
    solution = jnp.zeros_like(right_side)
    residual = right_side
    direction = right_side
    norm_now = jnp.sum(residual * residual, axis=1, keepdims=True)
    for iteration in range(step_count):
        mapped = operator(direction)
        stride = norm_now / jnp.sum(direction * mapped, axis=1, keepdims=True)
        solution = solution + stride * direction
        residual = residual - stride * mapped
        norm_next = jnp.sum(residual * residual, axis=1, keepdims=True)
        direction = residual + norm_next / norm_now * direction
        norm_now = norm_next
    return solution


def body(item_factors, exposure, confidence, tile_items, tile_users, tile_count):
    conf_tiles = confidence[0]
    item_row = tile_items[0]
    user_row = tile_users[0]
    live_count = tile_count[0]
    tile_total = conf_tiles.shape[0]
    block_size = conf_tiles.shape[1]
    rank_width = item_factors.shape[1]
    all_factors, all_exposure = (
        lax.all_gather(item_factors, "blk", axis=0, tiled=True),
        lax.all_gather(exposure, "blk", axis=0, tiled=True),
    )
    gram_items = lax.psum(weighted_gram(item_factors, exposure), "blk")
    factor_blocks = all_factors.reshape(tile_total, block_size, rank_width)
    exposure_blocks = all_exposure.reshape(tile_total, block_size)
    tile_factors = factor_blocks[item_row]
    tile_exposure = exposure_blocks[item_row].astype(jnp.float32)
    active = jnp.arange(tile_total, dtype=jnp.int32) < live_count
    conf_live = jnp.where(active[:, None, None], conf_tiles, jnp.zeros_like(conf_tiles))
    excess = jnp.where(
        conf_live > 0, conf_live.astype(jnp.float32) - tile_exposure[:, None, :], 0.0
    )
    member = (user_row[:, None] == jnp.arange(UB_DEV, dtype=jnp.int32)[None, :]).astype(jnp.float32)
    member_narrow = member.astype(jnp.bfloat16)
    tile_right = jnp.einsum(
        "tui,tik->tuk", conf_live, tile_factors, preferred_element_type=jnp.float32
    )
    user_right = jnp.einsum("tb,tuk->buk", member, tile_right, precision=FULL_PRECISION).reshape(
        -1, rank_width
    )

    def user_operator(direction):
        rounded = direction.astype(jnp.bfloat16).reshape(UB_DEV, block_size, rank_width)
        picked = jnp.einsum(
            "tb,buk->tuk", member_narrow, rounded, preferred_element_type=jnp.float32
        ).astype(jnp.bfloat16)
        scores = jnp.einsum(
            "tuk,tik->tui", picked, tile_factors, preferred_element_type=jnp.float32
        )
        weighted = (excess * scores).astype(jnp.bfloat16)
        returned = jnp.einsum(
            "tui,tik->tuk", weighted, tile_factors, preferred_element_type=jnp.float32
        )
        summed = jnp.einsum("tb,tuk->buk", member, returned, precision=FULL_PRECISION).reshape(
            -1, rank_width
        )
        return (
            LAMBDA * direction + jnp.dot(direction, gram_items, precision=FULL_PRECISION) + summed
        )

    user_factors = conjugate(user_right, user_operator, CG_STEPS).astype(jnp.bfloat16)
    local_gram = lax.dot_general(
        user_factors, user_factors, (((0,), (0,)), ((), ())), preferred_element_type=jnp.float32
    )
    gram_users = lax.psum(local_gram, ("blk", "grp"))
    user_gram = gram_users * (1.0 / (UB_DEV * block_size))
    tile_ids = jnp.arange(tile_total, dtype=jnp.int32)
    by_owner = jnp.zeros((tile_total,), jnp.int32).at[item_row].set(tile_ids)
    send_conf = conf_live[by_owner]
    send_active = active[by_owner]
    owner_member = member_narrow[by_owner]
    user_blocks = user_factors.reshape(UB_DEV, block_size, rank_width)
    send_rows = jnp.einsum(
        "tb,buk->tuk", owner_member, user_blocks, preferred_element_type=jnp.float32
    ).astype(jnp.bfloat16)
    send_rows = jnp.where(send_active[:, None, None], send_rows, jnp.zeros_like(send_rows))
    got_rows, got_conf = (
        lax.all_to_all(send_rows, ("blk", "grp"), split_axis=0, concat_axis=0, tiled=True),
        lax.all_to_all(send_conf, ("blk", "grp"), split_axis=0, concat_axis=0, tiled=True),
    )
    own_exposure = lax.dynamic_slice_in_dim(
        exposure, lax.axis_index("grp") * block_size, block_size
    ).astype(jnp.float32)
    item_excess = jnp.where(
        got_conf > 0, got_conf.astype(jnp.float32) - own_exposure[None, None, :], 0.0
    )
    contract_both = (((0, 1), (0, 1)), ((), ()))
    item_right = lax.dot_general(
        got_conf, got_rows, contract_both, preferred_element_type=jnp.float32
    )

    def item_operator(direction):
        rounded = direction.astype(jnp.bfloat16)
        scores = jnp.einsum("suk,ik->sui", got_rows, rounded, preferred_element_type=jnp.float32)
        weighted = (item_excess * scores).astype(jnp.bfloat16)
        returned = lax.dot_general(
            weighted, got_rows, contract_both, preferred_element_type=jnp.float32
        )
        gram_term = jnp.dot(direction, user_gram, precision=FULL_PRECISION)
        return LAMBDA * direction + own_exposure[:, None] * gram_term + returned

    item_scale = float(tile_total) ** 0.5
    item_update = (conjugate(item_right, item_operator, CG_STEPS) * item_scale).astype(jnp.bfloat16)
    return (user_factors, item_update, user_gram)


def solution(mesh):
    placed = (
        P("blk", None),
        P("blk"),
        P(("blk", "grp"), None, None, None),
        P(("blk", "grp"), None),
        P(("blk", "grp"), None),
        P(("blk", "grp")),
    )
    return jax.shard_map(
        body,
        mesh=mesh,
        in_specs=placed,
        out_specs=(P(("blk", "grp"), None), P(("blk", "grp"), None), P()),
        check_vma=False,
    )
```

profile of v0, /device:TPU:15, one launch (start us, length us, event | category | flops | bytes accessed | tf_op | source)
XLA Modules:
  0.0 940.8 jit_solution(14655493409501032757)
XLA Ops:
  7.2 0.7 all-gather.3.cloned.1.call-update
  8.5 0.7 fusion.108
  9.2 1.0 scatter_custom_fusion
  10.2 4.5 bitcast_select_fusion
  14.7 5.3 gather_fusion.2
  19.9 11.1 %all-to-all-start = ((bf16[128,128,128]{2,1,0:T(8,128)(2,1)}), bf16[128,128,128]{2,1,0:T(8,128)(2,1)}, u32[]{:S(2)}, u32[]{:S(2)}) async-start(bf16[128,128,128]{2,1,0:T(8,128)(2,1)} %gather_fusion.2), calls=%async_computation | async-start | bytes 8388608 | tf_op jit(solution)/shard_map/all_to_all | solution.py:104
  31.2 1.4 fusion.72
  32.6 1.2 gather_fusion.3
  33.8 102.3 %all-gather = bf16[32,1,512]{2,1,0:T(2,128)(2,1)S(1)} all-gather(bf16[1,1,512]{2,1,0:T(2,128)(2,1)S(1)} %reshape.201), channel_id=1, replica_groups=mesh['blk'=32,'grp'=4] {'blk'}, dimensions={0}, use_global_device_ids=true | all-gather | bytes 33792 | tf_op jit(solution)/shard_map/all_gather | solution.py:46
  136.3 0.7 gather_fusion.1
  137.1 0.7 gather_fusion.4
  137.9 54.2 %all-gather.3.cloned.1.call-done = bf16[16384,256]{1,0:T(8,128)(2,1)} async-done(((bf16[512,256]{1,0:T(8,128)(2,1)}), bf16[16384,256]{1,0:T(8,128)(2,1)}) %all-gather.3.cloned.1.call-update) | async-done | bytes 8388624 | tf_op jit(solution)/shard_map/all_gather | solution.py:45
  192.0 10.1 %gather_fusion = bf16[128,128,256]{2,1,0:T(8,128)(2,1)} fusion(bf16[128,128,256]{2,1,0:T(8,128)(2,1)} %bitcast.99, s32[1024]{0:T(1024)S(1)} %pad_clamp_fusion.1), kind=kCustom, calls=%fused_computation | custom fusion | bytes 16777728 | tf_op jit(solution)/shard_map/gather | solution.py:51
  202.2 7.0 fusion.125
  209.2 15.7 %multiply_reduce_fusion.4 = (f32[4,128]{0,1:T(8,128)S(1)}, f32[4,128,256]{2,0,1:T(4,128)S(1)}) fusion(f32[128,128,256]{2,1,0:T(8,128)S(1)} %fusion.125, s32[128]{0:T(128)S(1)} %bitcast.107), kind=kOutput, calls=%fused_computation.95 | convolution fusion | flops 201588736 | bytes 17304064 | tf_op jit(solution)/shard_map/tb,tuk->buk/dot_general | solution.py:63
  225.0 5.6 convolution_convert_fusion.2
  230.5 25.3 %fusion.14 = f32[128,128,256]{2,1,0:T(8,128)} fusion(bf16[128,128,256]{2,1,0:T(8,128)(2,1)} %gather_fusion, bf16[128,128,128]{2,1,0:T(8,128)(2,1)} %bitcast_select_fusion, f32[128,128]{1,0:T(8,128)S(1)} %convert_element_type.86, bf16[128,128,256]{2,0,1:T(8,128)(2,1)} %convolution_convert_fusion.2), kind=kOutput, calls=%fused_computation.32 | convolution fusion | flops 2160066560 | bytes 37814272 | tf_op jit(solution)/shard_map/tui,tik->tuk/dot_general | solution.py:76
  255.9 20.2 %fusion.4 = f32[4,128,256]{2,0,1:T(4,128)S(1)} fusion(f32[128,128,256]{2,1,0:T(8,128)} %fusion.14, s32[128]{0:T(128)S(1)} %bitcast.109), kind=kOutput, calls=%fused_computation.10 | convolution fusion | flops 201327104 | bytes 17302016 | tf_op jit(solution)/shard_map/tb,tuk->buk/dot_general | solution.py:79
  276.3 220.5 %all-reduce.3.cloned.1.call-done = f32[256,256]{1,0:T(8,128)} async-done(((f32[256,256]{1,0:T(8,128)}), f32[256,256]{1,0:T(8,128)}) %all-reduce.3.cloned.1.call-update) | async-done | bytes 262160 | tf_op jit(solution)/shard_map/psum | solution.py:48
  496.8 1.6 multiply_reduce_fusion.3
  498.4 0.2 multiply_reduce_fusion.2
  498.8 5.6 convolution_convert_fusion.1
  504.4 25.7 %fusion.15 = f32[128,128,256]{2,1,0:T(8,128)} fusion(bf16[128,128,256]{2,1,0:T(8,128)(2,1)} %gather_fusion, bf16[128,128,128]{2,1,0:T(8,128)(2,1)} %bitcast_select_fusion, f32[128,128]{1,0:T(8,128)S(1)} %convert_element_type.86, bf16[128,128,256]{2,0,1:T(8,128)(2,1)} %convolution_convert_fusion.1), kind=kOutput, calls=%fused_computation.33 | convolution fusion | flops 2160066560 | bytes 37814272 | tf_op jit(solution)/shard_map/tui,tik->tuk/dot_general | solution.py:76
  530.1 20.0 %fusion.2 = f32[4,128,256]{2,0,1:T(4,128)S(1)} fusion(f32[128,128,256]{2,1,0:T(8,128)} %fusion.15, s32[128]{0:T(128)S(1)} %bitcast.111), kind=kOutput, calls=%fused_computation.8 | convolution fusion | flops 201327104 | bytes 17302016 | tf_op jit(solution)/shard_map/tb,tuk->buk/dot_general | solution.py:79
  550.3 0.7 multiply_reduce_fusion.1
  551.0 0.2 multiply_reduce_fusion
  551.2 0.2 fusion.123
  551.4 5.6 convolution_convert_fusion
  557.0 25.5 %fusion.16 = f32[128,128,256]{2,1,0:T(8,128)} fusion(bf16[128,128,256]{2,1,0:T(8,128)(2,1)} %gather_fusion, bf16[128,128,128]{2,1,0:T(8,128)(2,1)} %bitcast_select_fusion, f32[128,128]{1,0:T(8,128)S(1)} %convert_element_type.86, bf16[128,128,256]{2,0,1:T(8,128)(2,1)} %convolution_convert_fusion), kind=kOutput, calls=%fused_computation.34 | convolution fusion | flops 2160066560 | bytes 37814272 | tf_op jit(solution)/shard_map/tui,tik->tuk/dot_general | solution.py:76
  582.5 20.2 %fusion = f32[4,128,256]{2,0,1:T(4,128)S(1)} fusion(f32[128,128,256]{2,1,0:T(8,128)} %fusion.16, s32[128]{0:T(128)S(1)} %bitcast.113), kind=kOutput, calls=%fused_computation.6 | convolution fusion | flops 201327104 | bytes 17302016 | tf_op jit(solution)/shard_map/tb,tuk->buk/dot_general | solution.py:79
  602.8 0.7 fusion.60
  603.5 0.3 add_convert_fusion
  603.8 5.5 convert_select_fusion
  609.3 11.4 %copy.86 = bf16[128,128,256]{2,1,0:T(8,128)(2,1)} copy(bf16[128,128,256]{2,0,1:T(8,128)(2,1)} %convert_select_fusion) | data formatting | bytes 16777216 | tf_op jit(solution)/shard_map/jit(_where)/select_n | solution.py:101
  620.7 45.2 %all-to-all-start.1 = ((bf16[128,128,256]{2,1,0:T(8,128)(2,1)}), bf16[128,128,256]{2,1,0:T(8,128)(2,1)}, u32[]{:S(2)}, u32[]{:S(2)}) async-start(bf16[128,128,256]{2,1,0:T(8,128)(2,1)} %copy.86), calls=%async_computation.1 | async-start | bytes 16777216 | tf_op jit(solution)/shard_map/all_to_all | solution.py:103
  665.9 0.3 all-reduce.5.cloned.1.call-start
  666.2 1.0 fusion.126
  667.3 219.2 %all-reduce.5.cloned.1.call-done = f32[256,256]{1,0:T(8,128)} async-done(((f32[256,256]{1,0:T(8,128)}), f32[256,256]{1,0:T(8,128)}) %all-reduce.5.cloned.1.call-update) | async-done | bytes 262160 | tf_op jit(solution)/shard_map/psum | solution.py:90
  886.4 1.0 broadcast_multiply_fusion
  887.4 6.3 convolution_bitcast_fusion
  893.7 12.4 %fusion.70 = f32[128,256]{1,0:T(8,128)S(1)} fusion(bf16[128,128,256]{2,1,0:T(8,128)(2,1)} %all-to-all-done.1, bf16[128,128,128]{2,1,0:T(8,128)(2,1)} %all-to-all-done, f32[128]{0:T(128)S(1)} %dynamic-slice_convert_fusion, f32[128,256]{1,0:T(8,128)S(1)} %convolution_bitcast_fusion), kind=kOutput, calls=%fused_computation.81 | convolution fusion | flops 2160099328 | bytes 12845568 | tf_op jit(solution)/shard_map/dot_general | solution.py:121
  906.1 0.4 multiply_reduce_fusion.8
  906.8 12.4 %fusion.69 = f32[128,256]{1,0:T(8,128)S(1)} fusion(bf16[128,128,256]{2,1,0:T(8,128)(2,1)} %all-to-all-done.1, bf16[128,128,128]{2,1,0:T(8,128)(2,1)} %all-to-all-done, f32[128]{0:T(128)S(1)} %dynamic-slice_convert_fusion, f32[128,256]{1,0:T(8,128)S(1)} %multiply_add_fusion.3), kind=kOutput, calls=%fused_computation.80 | convolution fusion | flops 2160099328 | bytes 12845568 | tf_op jit(solution)/shard_map/dot_general | solution.py:121
  919.2 0.4 multiply_reduce_fusion.6
  919.6 0.2 multiply_reduce_fusion.5
  919.9 12.7 %fusion.68 = f32[128,256]{1,0:T(8,128)S(1)} fusion(bf16[128,128,256]{2,1,0:T(8,128)(2,1)} %all-to-all-done.1, bf16[128,128,128]{2,1,0:T(8,128)(2,1)} %all-to-all-done, f32[128]{0:T(128)S(1)} %dynamic-slice_convert_fusion, f32[128,256]{1,0:T(8,128)S(1)} %multiply_add_fusion.2), kind=kOutput, calls=%fused_computation.79 | convolution fusion | flops 2160099328 | bytes 12845568 | tf_op jit(solution)/shard_map/dot_general | solution.py:121
  932.6 0.4 fusion.71
  933.0 0.8 multiply_convert_fusion.18
  (49 shorter events, 1.6 us)
Async XLA Ops:
  7.2 184.9 %all-gather.3.cloned.1.call-start = ((), (), s32[]{:S(2)}) async-start(), calls=%async_computation.2 | async-start | bytes 8650752 | tf_op jit(solution)/shard_map/all_gather | solution.py:45
  14.7 16.5 %copy-start.5 = (bf16[512]{0:T(512)(128)(2,1)S(1)}, bf16[512]{0:T(512)(128)(2,1)}, u32[]{:S(2)}) copy-start(bf16[512]{0:T(512)(128)(2,1)} %param.7) | copy-start | bytes 3076
  14.7 16.5 %copy-start.1 = (bf16[512,256]{1,0:T(8,128)(2,1)S(1)}, bf16[512,256]{1,0:T(8,128)(2,1)}, u32[]{:S(2)}) copy-start(bf16[512,256]{1,0:T(8,128)(2,1)} %param.6) | copy-start | bytes 786436
  14.7 122.4 %copy-start.4 = (s32[1,128]{1,0:T(1,128)S(1)}, s32[1,128]{1,0:T(1,128)}, u32[]{:S(2)}) copy-start(s32[1,128]{1,0:T(1,128)} %param.10) | copy-start | bytes 1540
  19.9 600.7 %all-to-all-start = ((bf16[128,128,128]{2,1,0:T(8,128)(2,1)}), bf16[128,128,128]{2,1,0:T(8,128)(2,1)}, u32[]{:S(2)}, u32[]{:S(2)}) async-start(bf16[128,128,128]{2,1,0:T(8,128)(2,1)} %gather_fusion.2), calls=%async_computation | async-start | bytes 8388608 | tf_op jit(solution)/shard_map/all_to_all | solution.py:104
  31.1 465.7 %all-reduce.3.cloned.1.call-start = ((), (), s32[]{:S(2)}) async-start(), calls=%async_computation.3 | async-start | bytes 524288 | tf_op jit(solution)/shard_map/psum | solution.py:48
  530.1 20.2 %copy-start.3 = (f32[256,256]{1,0:T(8,128)S(1)}, f32[256,256]{1,0:T(8,128)}, u32[]{:S(2)}) copy-start(f32[256,256]{1,0:T(8,128)} %all-reduce.3.cloned.1.call-done) | copy-start | bytes 786436
  603.8 62.4 %copy-start.2 = (bf16[512,256]{1,0:T(8,128)(2,1)}, bf16[512,256]{1,0:T(8,128)(2,1)S(1)}, u32[]{:S(2)}) copy-start(bf16[512,256]{1,0:T(8,128)(2,1)S(1)} %add_convert_fusion) | copy-start | bytes 786436
  620.7 266.7 %all-to-all-start.1 = ((bf16[128,128,256]{2,1,0:T(8,128)(2,1)}), bf16[128,128,256]{2,1,0:T(8,128)(2,1)}, u32[]{:S(2)}, u32[]{:S(2)}) async-start(bf16[128,128,256]{2,1,0:T(8,128)(2,1)} %copy.86), calls=%async_computation.1 | async-start | bytes 16777216 | tf_op jit(solution)/shard_map/all_to_all | solution.py:103
  665.9 220.6 %all-reduce.5.cloned.1.call-start = ((), (), s32[]{:S(2)}) async-start(), calls=%async_computation.4 | async-start | bytes 524288 | tf_op jit(solution)/shard_map/psum | solution.py:90
  887.4 45.2 %copy-start = (f32[256,256]{1,0:T(8,128)}, f32[256,256]{1,0:T(8,128)S(1)}, u32[]{:S(2)}) copy-start(f32[256,256]{1,0:T(8,128)S(1)} %broadcast_multiply_fusion) | copy-start | bytes 786436
Sparse Core Ops, SparseCore 0:
  9.6 182.3 all-gather.2
  195.1 301.6 all-reduce.2
  672.8 213.6 all-reduce.4
where the time goes:
time: 948 us; the launch traced here: 941 us
  waiting for transfers between devices  495 us (52%)
  matrix products  232 us (24%)
  blocking collectives  102 us (11%)
  starting transfers between devices  56.7 us (6%)
  local copies, waits for them, and re-layouts  30.9 us (3%)
  between operations  15.3 us (2%)
    psum x1, waiting for transfers between devices, body(): gram_items = lax.psum(weighted_gram(item_factors, exposure), 'blk')  220 us
    psum x1, waiting for transfers between devices, body(): gram_users = lax.psum(local_gram, ('blk', 'grp'))  219 us
    all_gather x1, blocking collectives, body(): lax.all_gather(exposure, 'blk', axis=0, tiled=True)  102 us
    dot_general x3, matrix products, user_operator(): jnp.einsum('tui,tik->tuk', weighted, tile_factors, preferred_element_type...  76.5 us
    dot_general x3, matrix products, user_operator(): jnp.einsum('tb,tuk->buk', member, returned, precision=FULL_PRECISION)  60.4 us
    all_gather x1, waiting for transfers between devices, body(): lax.all_gather(item_factors, 'blk', axis=0, tiled=True)  54.2 us
    all_to_all x1, starting transfers between devices, body(): lax.all_to_all(send_rows, ('blk', 'grp'), split_axis=0, concat_axis=0, ti...  45.2 us
    dot_general x3, matrix products, item_operator(): lax.dot_general(weighted, got_rows, contract_both, preferred_element_type...  37.5 us
  transfers between devices with their start and end apart: 5, of which 3 were waited for; matrix products, arithmetic and copies ran while one was open for 24% of the time, Pallas kernels for 0%

commit v1 on v0

v1 whole, which is shorter than its diff:
```python
import functools

import jax
import jax.numpy as jnp
from jax import lax
from jax.experimental import pallas as pl
from jax.experimental.pallas import tpu as pltpu
from jax.sharding import PartitionSpec as P

UB = 4
BS = 128
RANK = 256
TILES = 128
STEPS = 3
GROUP = 4
SLOTS = TILES + UB * GROUP
HIGH = lax.Precision.HIGHEST
BF = jnp.bfloat16
F32 = jnp.float32
VMEM_BYTES = 56 * 1024 * 1024
BOTH = ("blk", "grp")


def nt(a, b):
    return lax.dot_general(a, b, (((1,), (1,)), ((), ())), preferred_element_type=F32)


def nn(a, b):
    return lax.dot_general(a, b, (((1,), (0,)), ((), ())), preferred_element_type=F32)


def tn(a, b):
    return lax.dot_general(a, b, (((0,), (0,)), ((), ())), preferred_element_type=F32)


def row_sum(v):
    return jnp.sum(v, axis=1, keepdims=True)


def send_kernel(items, count, conf, out):
    def one(t, carry):
        tile = conf[t]
        tile = jnp.where(t < count[0], tile, jnp.zeros_like(tile))
        out[items[t]] = tile.T
        return carry

    lax.fori_loop(0, TILES, one, 0, unroll=4)


def send_conf_of(items, count, conf):
    smem = pl.BlockSpec(memory_space=pltpu.SMEM)
    vmem = pl.BlockSpec(memory_space=pltpu.VMEM)
    return pl.pallas_call(
        send_kernel,
        out_shape=jax.ShapeDtypeStruct((TILES, BS, BS), BF),
        in_specs=[smem, smem, vmem],
        out_specs=vmem,
        compiler_params=pltpu.CompilerParams(vmem_limit_bytes=VMEM_BYTES),
        name="send_conf",
    )(items, count, conf)


def user_kernel(
    items, users, count, conf_hbm, factors_hbm, exposure,
    out, rows_hbm, gram_out,
    conf, factors, slots, heads, gram, right, direction, narrow, mapped, answer, residual, sems,
):
    conf_copy = pltpu.make_async_copy(conf_hbm, conf.at[pl.ds(0, TILES)], sems.at[0])
    factor_copy = pltpu.make_async_copy(factors_hbm, factors, sems.at[1])
    factor_copy.start()
    conf_copy.start()
    conf[TILES] = jnp.zeros((BS, BS), BF)
    live = count[0]

    for b in range(UB):
        heads[b] = 0

    def tally(t, carry):
        b = users[t]
        heads[b] = heads[b] + 1
        return carry

    lax.fori_loop(0, live, tally, 0)
    ends = []
    begin = jnp.int32(0)
    for b in range(UB):
        size = heads[b]
        heads[b] = begin
        begin = begin + (size + GROUP - 1) // GROUP * GROUP
        ends.append(begin)
    total = ends[-1]

    def blank(s, carry):
        slots[s] = TILES
        return carry

    lax.fori_loop(0, total, blank, 0)

    def place(t, carry):
        b = users[t]
        s = heads[b]
        slots[s] = t
        heads[b] = s + 1
        return carry

    lax.fori_loop(0, live, place, 0)

    factor_copy.wait()

    def gram_step(p, carry):
        pair = factors[pl.ds(pl.multiple_of(p * 2 * BS, 2 * BS), 2 * BS), :]
        weights = jnp.concatenate(
            [exposure[pl.ds(2 * p, 1), :], exposure[pl.ds(2 * p + 1, 1), :]], axis=1
        )
        scaled = pair.astype(F32).T * weights
        high = scaled.astype(BF)
        low = (scaled - high.astype(F32)).astype(BF)
        return carry + nn(high, pair) + nn(low, pair)

    gram[...] = jnp.zeros_like(gram)

    def gram_four(p, carry):
        sub = gram_step(2 * p, 0.0) + gram_step(2 * p + 1, 0.0)
        gram[...] += sub
        return carry

    lax.fori_loop(0, TILES // 4, gram_four, 0)
    conf_copy.wait()

    def group_of(g):
        first = g * GROUP
        b = (
            (first >= ends[0]).astype(jnp.int32)
            + (first >= ends[1]).astype(jnp.int32)
            + (first >= ends[2]).astype(jnp.int32)
        )
        confs, parts, levels = [], [], []
        for j in range(GROUP):
            t = slots[first + j]
            item = items[jnp.minimum(t, TILES - 1)]
            confs.append(conf[t])
            parts.append(factors[pl.ds(pl.multiple_of(item * BS, BS), BS), :])
            levels.append(exposure[pl.ds(item, 1), :])
        rows = pl.ds(pl.multiple_of(b * BS, BS), BS)
        return rows, jnp.concatenate(confs, axis=1), jnp.concatenate(parts, axis=0), levels

    right[...] = jnp.zeros_like(right)

    def right_step(g, carry):
        rows, weights, parts, _ = group_of(g)
        right[rows, :] += nn(weights, parts)
        return carry

    groups = total // GROUP
    lax.fori_loop(0, groups, right_step, 0)

    def map_step(g, carry):
        rows, weights, parts, levels = group_of(g)
        wide = weights.astype(F32)
        excess = jnp.where(wide > 0, wide - jnp.concatenate(levels, axis=1), 0.0)
        scores = nt(narrow[rows, :], parts)
        mapped[rows, :] += nn((excess * scores).astype(BF), parts)
        return carry

    residual[...] = right[...]
    direction[...] = right[...]
    answer[...] = jnp.zeros_like(answer)
    norm = row_sum(right[...] * right[...])
    for step in range(STEPS):
        way = direction[...]
        narrow[...] = way.astype(BF)
        mapped[...] = way + jnp.dot(way, gram[...], precision=HIGH, preferred_element_type=F32)
        lax.fori_loop(0, groups, map_step, 0)
        image = mapped[...]
        stride = norm / row_sum(way * image)
        answer[...] += stride * way
        if step < STEPS - 1:
            rest = residual[...] - stride * image
            residual[...] = rest
            norm_next = row_sum(rest * rest)
            direction[...] = rest + norm_next / norm * way
            norm = norm_next

    result = answer[...].astype(BF)
    out[...] = result

    def send_row(t, carry):
        rows = pl.ds(pl.multiple_of(users[t] * BS, BS), BS)
        pltpu.make_async_copy(out.at[rows, :], rows_hbm.at[items[t]], sems.at[2]).start()
        return carry

    lax.fori_loop(0, TILES, send_row, 0)
    gram_out[...] = tn(result, result)
    pltpu.make_async_copy(rows_hbm, rows_hbm, sems.at[2]).wait()


def user_half(items, users, count, conf, factors, exposure):
    smem = pl.BlockSpec(memory_space=pltpu.SMEM)
    vmem = pl.BlockSpec(memory_space=pltpu.VMEM)
    far = pl.BlockSpec(memory_space=pl.ANY)
    wide = pltpu.VMEM((UB * BS, RANK), F32)
    return pl.pallas_call(
        user_kernel,
        out_shape=(
            jax.ShapeDtypeStruct((UB * BS, RANK), BF),
            jax.ShapeDtypeStruct((TILES, BS, RANK), BF),
            jax.ShapeDtypeStruct((RANK, RANK), F32),
        ),
        in_specs=[smem, smem, smem, far, far, vmem],
        out_specs=(vmem, far, vmem),
        scratch_shapes=[
            pltpu.VMEM((TILES + 1, BS, BS), BF),
            pltpu.VMEM((TILES * BS, RANK), BF),
            pltpu.SMEM((SLOTS,), jnp.int32),
            pltpu.SMEM((UB,), jnp.int32),
            pltpu.VMEM((RANK, RANK), F32),
            wide,
            wide,
            pltpu.VMEM((UB * BS, RANK), BF),
            wide,
            wide,
            wide,
            pltpu.SemaphoreType.DMA((3,)),
        ],
        compiler_params=pltpu.CompilerParams(vmem_limit_bytes=VMEM_BYTES),
        name="user_half",
    )(items, users, count, conf, factors, exposure)


ITEM_GROUP = 8


def item_kernel(
    conf_hbm, rows_hbm, exposure, user_gram,
    out,
    conf, rows, mapped, narrow, sems,
):
    chunk = ITEM_GROUP
    chunks = TILES // chunk
    copies = []
    for c in range(chunks):
        part = pl.ds(c * chunk, chunk)
        copies.append(
            (
                pltpu.make_async_copy(rows_hbm.at[part], rows.at[part], sems.at[0, c]),
                pltpu.make_async_copy(conf_hbm.at[part], conf.at[part], sems.at[1, c]),
            )
        )
    for pair in copies:
        pair[0].start()
        pair[1].start()
    level = jnp.broadcast_to(exposure[...], (BS, BS)).T
    level_wide = jnp.concatenate([level] * chunk, axis=1)
    level_rank = jnp.concatenate([level] * (RANK // BS), axis=1)

    def chunk_of(c):
        weights = jnp.concatenate([conf[c * chunk + j] for j in range(chunk)], axis=1)
        part = rows[pl.ds(c * chunk, chunk)].reshape(chunk * BS, RANK)
        return weights, part

    mapped[...] = jnp.zeros_like(mapped)
    for c in range(chunks):
        copies[c][0].wait()
        copies[c][1].wait()
        weights, part = chunk_of(c)
        mapped[...] += nn(weights, part)
    right = mapped[...]

    def map_step(c, carry):
        weights, part = chunk_of(c)
        wide = weights.astype(F32)
        excess = jnp.where(wide > 0, wide - level_wide, 0.0)
        scores = nt(narrow[...], part)
        mapped[...] += nn((excess * scores).astype(BF), part)
        return carry

    residual = right
    way = right
    answer = jnp.zeros_like(right)
    norm = row_sum(right * right)
    for step in range(STEPS):
        narrow[...] = way.astype(BF)
        term = jnp.dot(way, user_gram[...], precision=HIGH, preferred_element_type=F32)
        mapped[...] = way + level_rank * term
        lax.fori_loop(0, chunks, map_step, 0)
        image = mapped[...]
        stride = norm / row_sum(way * image)
        answer = answer + stride * way
        if step < STEPS - 1:
            residual = residual - stride * image
            norm_next = row_sum(residual * residual)
            way = residual + norm_next / norm * way
            norm = norm_next
    out[...] = (answer * (float(TILES) ** 0.5)).astype(BF)


def item_half(conf, rows, exposure, user_gram):
    vmem = pl.BlockSpec(memory_space=pltpu.VMEM)
    far = pl.BlockSpec(memory_space=pl.ANY)
    return pl.pallas_call(
        item_kernel,
        out_shape=jax.ShapeDtypeStruct((BS, RANK), BF),
        in_specs=[far, far, vmem, vmem],
        out_specs=vmem,
        scratch_shapes=[
            pltpu.VMEM((TILES, BS, BS), BF),
            pltpu.VMEM((TILES, BS, RANK), BF),
            pltpu.VMEM((BS, RANK), F32),
            pltpu.VMEM((BS, RANK), BF),
            pltpu.SemaphoreType.DMA((2, TILES // ITEM_GROUP)),
        ],
        compiler_params=pltpu.CompilerParams(vmem_limit_bytes=VMEM_BYTES),
        name="item_half",
    )(conf, rows, exposure, user_gram)


def exchange(values, axes):
    return lax.all_to_all(values, axes, split_axis=0, concat_axis=0, tiled=True)


def body(item_factors, exposure, confidence, tile_items, tile_users, tile_count):
    conf_tiles = confidence[0]
    items = tile_items[0]
    users = tile_users[0]
    panels = lax.axis_size("blk")
    size = item_factors.shape[0]
    extra = 16
    tail = jnp.pad(exposure.reshape(-1, RANK), ((0, extra - size // RANK), (0, 0)))
    packed = jnp.concatenate([item_factors, tail], axis=0)
    gathered = exchange(
        jnp.broadcast_to(packed[None], (panels, size + extra, RANK)).reshape(-1, RANK), "blk"
    ).reshape(panels, size + extra, RANK)
    factors = gathered[:, :size].reshape(panels * size, RANK)
    levels = gathered[:, size : size + size // RANK].reshape(TILES, BS).astype(F32)
    send_conf = send_conf_of(items, tile_count, conf_tiles)
    got_conf = exchange(send_conf, BOTH)
    user_factors, send_rows, local_gram = user_half(
        items, users, tile_count, conf_tiles, factors, levels
    )
    got_rows = exchange(send_rows, BOTH)
    pieces = exchange(local_gram.reshape(TILES, -1, RANK), BOTH)
    mine = jnp.sum(pieces, axis=0) * (1.0 / (UB * BS))
    user_gram = exchange(
        jnp.broadcast_to(mine[None], (TILES,) + mine.shape), BOTH
    ).reshape(RANK, RANK)
    own = lax.dynamic_slice_in_dim(exposure, lax.axis_index("grp") * BS, BS)
    item_update = item_half(got_conf, got_rows, own.astype(F32).reshape(1, BS), user_gram)
    return user_factors, item_update, user_gram


def solution(mesh):
    placed = (
        P("blk", None),
        P("blk"),
        P(BOTH, None, None, None),
        P(BOTH, None),
        P(BOTH, None),
        P(BOTH),
    )
    return jax.shard_map(
        body,
        mesh=mesh,
        in_specs=placed,
        out_specs=(P(BOTH, None), P(BOTH, None), P()),
        check_vma=False,
    )
```

time: 948 us -> 462 us (0.49)
  matrix products: 232 us -> 0 us
  waiting for transfers between devices: 495 us -> 281 us
  blocking collectives: 102 us -> 15.9 us
  Pallas kernels: 0 us -> 82.9 us
  local copies, waits for them, and re-layouts: 30.9 us -> 15.5 us
  between operations: 15.3 us -> 1.51 us
    psum x2 -> x0, waiting for transfers between devices: 440 us -> none  [the longest x1 220 us: body(): gram_items = lax.psum(weighted_gram(item_factors, exposure), 'blk')]
    all_to_all x2 -> x4, waiting for transfers between devices: 0.01 us -> 281 us  [exchange(): return lax.all_to_all(values, axes, split_axis=0, concat_axis=0, tiled=True)]
    dot_general x24 -> x0, matrix products: 232 us -> none  [the longest x3 76.5 us: user_operator(): jnp.einsum('tui,tik->tuk', weighted, tile_factors, preferred_element_type...]
    all_gather x1 -> x0, blocking collectives: 102 us -> none  [body(): lax.all_gather(exposure, 'blk', axis=0, tiled=True)]
    pallas_call x0 -> x3, Pallas kernels: none -> 82.9 us  [the longest x1 44.3 us: user_half(): pl.pallas_call(user_kernel, out_shape=(jax.ShapeDtypeStruct((UB * BS, RAN...]
    all_gather x1 -> x0, waiting for transfers between devices: 54.2 us -> none  [body(): lax.all_gather(item_factors, 'blk', axis=0, tiled=True)]
    gather x5 -> x0, local copies, waits for them, and re-layouts: 18.1 us -> none  [the longest x1 10.1 us: body(): tile_factors = factor_blocks[item_row]]
    all_to_all x0 -> x1, blocking collectives: none -> 15.9 us  [exchange(): return lax.all_to_all(values, axes, split_axis=0, concat_axis=0, tiled=True)]
  transfers between devices with their start and end apart: 5 -> 4, of which waited for: 3 -> 4; matrix products, arithmetic and copies ran while one was open for 24% -> 0% of each run, Pallas kernels for 0% -> 2%
where the time goes in v1:
time: 462 us; the launch traced here: 453 us
  waiting for transfers between devices  281 us (61%)
  Pallas kernels  82.9 us (18%)
  starting transfers between devices  54.3 us (12%)
  blocking collectives  15.9 us (3%)
  local copies, waits for them, and re-layouts  15.5 us (3%)
    all_to_all x4, waiting for transfers between devices, exchange(): return lax.all_to_all(values, axes, split_axis=0, concat_axis=0, tiled=True)  281 us
    all_to_all x4, starting transfers between devices, exchange(): return lax.all_to_all(values, axes, split_axis=0, concat_axis=0, tiled=True)  54.3 us
    pallas_call x1, Pallas kernels, user_half(): pl.pallas_call(user_kernel, out_shape=(jax.ShapeDtypeStruct((UB * BS, RAN...  44.3 us
    pallas_call x1, Pallas kernels, item_half(): pl.pallas_call(item_kernel, out_shape=jax.ShapeDtypeStruct((BS, RANK), BF...  31.4 us
    all_to_all x1, blocking collectives, exchange(): return lax.all_to_all(values, axes, split_axis=0, concat_axis=0, tiled=True)  15.9 us
  transfers between devices with their start and end apart: 4, of which 4 were waited for; matrix products, arithmetic and copies ran while one was open for 0% of the time, Pallas kernels for 2%

profile of v1, /device:TPU:15, one launch (start us, length us, event | category | flops | bytes accessed | tf_op | source)
XLA Modules:
  0.0 453.5 jit_solution(4002207714815895675)
XLA Ops:
  0.6 0.7 reshape.36
  1.3 1.0 fusion.1
  2.3 3.9 broadcast_in_dim.4
  6.2 8.9 %all-to-all-start = ((bf16[32,528,256]{2,1,0:T(8,128)(2,1)}), bf16[32,528,256]{2,1,0:T(8,128)(2,1)}, u32[]{:S(2)}, u32[]{:S(2)}) async-start(bf16[32,528,256]{2,1,0:T(8,128)(2,1)} %broadcast_in_dim.4), calls=%async_computation | async-start | bytes 17301504 | tf_op jit(solution)/shard_map/all_to_all | solution.py:318
  15.8 124.5 %all-to-all-done = bf16[32,528,256]{2,1,0:T(8,128)(2,1)} async-done(((bf16[32,528,256]{2,1,0:T(8,128)(2,1)}), bf16[32,528,256]{2,1,0:T(8,128)(2,1)}, u32[]{:S(2)}, u32[]{:S(2)}) %all-to-all-start) | async-done | bytes 8650784 | tf_op jit(solution)/shard_map/all_to_all | solution.py:318
  140.3 0.9 slice_convert_fusion
  141.2 0.7 reshape.42.exposure
  141.9 7.5 %slice.8 = bf16[32,512,256]{2,1,0:T(8,128)(2,1)} slice(bf16[32,528,256]{2,1,0:T(8,128)(2,1)} %all-to-all-done), slice={[0:32], [0:512], [0:256]} | slice | bytes 16777216 | tf_op jit(solution)/shard_map/slice | solution.py:333
  149.4 44.3 %user_half.1 = (bf16[512,256]{1,0:T(8,128)(2,1)}, bf16[128,128,256]{2,1,0:T(8,128)(2,1)}, f32[256,256]{1,0:T(8,128)}) custom-call(s32[128]{0:T(128)} %bitcast.10, s32[128]{0:T(128)} %bitcast.12, s32[1]{0:T(128)S(6)} %copy.9.count, bf16[128,128,128]{2,1,0:T(8,128)(2,1)} %bitcast.8, bf16[16384,256]{1,0:T(8,128)(2,1)} %bitcast.7, f32[128,128]{1,0:T(8,128)} %reshape.42.exposure), custom_call_target="tpu_custom_call" | custom-call | tf_op jit(solution)/shard_map/user_half/pallas_call | solution.py:202
  193.7 1.8 reshape.40
  195.5 27.1 %all-to-all-start.3 = ((f32[128,2,256]{2,1,0:T(2,128)}), f32[128,2,256]{2,1,0:T(2,128)S(1)}, u32[]{:S(2)}, u32[]{:S(2)}) async-start(f32[128,2,256]{2,1,0:T(2,128)} %reshape.40), calls=%async_computation.3 | async-start | bytes 524288 | tf_op jit(solution)/shard_map/all_to_all | solution.py:318
  222.5 7.3 %send_conf.1 = bf16[128,128,128]{2,1,0:T(8,128)(2,1)} custom-call(s32[128]{0:T(128)} %bitcast.11, s32[1]{0:T(128)S(6)} %copy.9.count, bf16[128,128,128]{2,1,0:T(8,128)(2,1)} %bitcast.9), custom_call_target="tpu_custom_call" | custom-call | tf_op jit(solution)/shard_map/send_conf/pallas_call | solution.py:53
  229.8 0.7 all-to-all-done.3
  230.6 9.5 %all-to-all-start.1 = ((bf16[128,128,128]{2,1,0:T(8,128)(2,1)}), bf16[128,128,128]{2,1,0:T(8,128)(2,1)}, u32[]{:S(2)}, u32[]{:S(2)}) async-start(bf16[128,128,128]{2,1,0:T(8,128)(2,1)} %send_conf.1), calls=%async_computation.1 | async-start | bytes 8388608 | tf_op jit(solution)/shard_map/all_to_all | solution.py:318
  240.1 0.1 reduce_sum.9
  240.2 51.2 %all-to-all-done.1.conf_hbm = bf16[128,128,128]{2,1,0:T(8,128)(2,1)} async-done(((bf16[128,128,128]{2,1,0:T(8,128)(2,1)}), bf16[128,128,128]{2,1,0:T(8,128)(2,1)}, u32[]{:S(2)}, u32[]{:S(2)}) %all-to-all-start.1) | async-done | bytes 4194336 | tf_op jit(solution)/shard_map/all_to_all | solution.py:318
  291.5 0.1 broadcast_in_dim.5
  291.5 15.9 %all_to_all.26 = f32[128,2,256]{2,1,0:T(2,128)S(1)} all-to-all(f32[128,2,256]{2,1,0:T(2,128)S(1)} %broadcast_in_dim.5), channel_id=1, replica_groups=mesh['blk'=32,'grp'=4] {'blk','grp'}, dimensions={0} | all-to-all | bytes 524288 | tf_op jit(solution)/shard_map/all_to_all | solution.py:318
  307.4 0.0 copy-start
  307.4 8.8 %all-to-all-start.2 = ((bf16[128,128,256]{2,1,0:T(8,128)(2,1)}), bf16[128,128,256]{2,1,0:T(8,128)(2,1)}, u32[]{:S(2)}, u32[]{:S(2)}) async-start(bf16[128,128,256]{2,1,0:T(8,128)(2,1)} %get-tuple-element.7), calls=%async_computation.2 | async-start | bytes 16777216 | tf_op jit(solution)/shard_map/all_to_all | solution.py:318
  316.2 0.0 copy-done
  316.2 0.6 bitcast_convert_fusion.exposure
  316.8 0.9 reshape.41.user_gram
  317.7 104.3 %all-to-all-done.2.rows_hbm = bf16[128,128,256]{2,1,0:T(8,128)(2,1)} async-done(((bf16[128,128,256]{2,1,0:T(8,128)(2,1)}), bf16[128,128,256]{2,1,0:T(8,128)(2,1)}, u32[]{:S(2)}, u32[]{:S(2)}) %all-to-all-start.2) | async-done | bytes 8388640 | tf_op jit(solution)/shard_map/all_to_all | solution.py:318
  422.0 31.4 %item_half.1 = bf16[128,256]{1,0:T(8,128)(2,1)} custom-call(bf16[128,128,128]{2,1,0:T(8,128)(2,1)} %all-to-all-done.1.conf_hbm, bf16[128,128,256]{2,1,0:T(8,128)(2,1)} %all-to-all-done.2.rows_hbm, f32[1,128]{1,0:T(1,128)} %bitcast_convert_fusion.exposure, f32[256,256]{1,0:T(8,128)} %reshape.41.user_gram), custom_call_target="tpu_custom_call" | custom-call | tf_op jit(solution)/shard_map/item_half/pallas_call | solution.py:300
  (1 shorter events, 0.0 us)
Async XLA Ops:
  6.2 134.1 %all-to-all-start = ((bf16[32,528,256]{2,1,0:T(8,128)(2,1)}), bf16[32,528,256]{2,1,0:T(8,128)(2,1)}, u32[]{:S(2)}, u32[]{:S(2)}) async-start(bf16[32,528,256]{2,1,0:T(8,128)(2,1)} %broadcast_in_dim.4), calls=%async_computation | async-start | bytes 17301504 | tf_op jit(solution)/shard_map/all_to_all | solution.py:318
  195.5 35.1 %all-to-all-start.3 = ((f32[128,2,256]{2,1,0:T(2,128)}), f32[128,2,256]{2,1,0:T(2,128)S(1)}, u32[]{:S(2)}, u32[]{:S(2)}) async-start(f32[128,2,256]{2,1,0:T(2,128)} %reshape.40), calls=%async_computation.3 | async-start | bytes 524288 | tf_op jit(solution)/shard_map/all_to_all | solution.py:318
  230.6 60.9 %all-to-all-start.1 = ((bf16[128,128,128]{2,1,0:T(8,128)(2,1)}), bf16[128,128,128]{2,1,0:T(8,128)(2,1)}, u32[]{:S(2)}, u32[]{:S(2)}) async-start(bf16[128,128,128]{2,1,0:T(8,128)(2,1)} %send_conf.1), calls=%async_computation.1 | async-start | bytes 8388608 | tf_op jit(solution)/shard_map/all_to_all | solution.py:318
  307.4 8.8 %copy-start = (bf16[512]{0:T(512)(128)(2,1)S(1)}, bf16[512]{0:T(512)(128)(2,1)}, u32[]{:S(2)}) copy-start(bf16[512]{0:T(512)(128)(2,1)} %param.7) | copy-start | bytes 3076
  307.4 114.6 %all-to-all-start.2 = ((bf16[128,128,256]{2,1,0:T(8,128)(2,1)}), bf16[128,128,256]{2,1,0:T(8,128)(2,1)}, u32[]{:S(2)}, u32[]{:S(2)}) async-start(bf16[128,128,256]{2,1,0:T(8,128)(2,1)} %get-tuple-element.7), calls=%async_computation.2 | async-start | bytes 16777216 | tf_op jit(solution)/shard_map/all_to_all | solution.py:318

commit v2 on v1

v2 whole, which is shorter than its diff:
```python
import functools

import jax
import jax.numpy as jnp
from jax import lax
from jax.experimental import pallas as pl
from jax.experimental.pallas import tpu as pltpu
from jax.sharding import PartitionSpec as P

UB = 4
BS = 128
RANK = 256
TILES = 128
STEPS = 3
GROUP = 8
BATCH = 3
SLOTS = TILES + (UB + BATCH) * GROUP
HIGH = lax.Precision.HIGHEST
BF = jnp.bfloat16
F32 = jnp.float32
VMEM_BYTES = 56 * 1024 * 1024
BOTH = ("blk", "grp")
SIDE = 4
XLO = 2
CORES = 2
HALF = 256
PART_A = 112
PART_B = HALF - PART_A
TAIL = 16
OFFSETS = (0, 1, -1, 2)


def place_of(x, y, z, core):
    panel = ((y % SIDE) * XLO + x % XLO) * SIDE + z % SIDE
    return panel * 4 + (x % SIDE) // XLO * CORES + core


def from_offset(dx=0, dy=0, dz=0, flip=0):
    return [
        (place_of(x + dx, y + dy, z + dz, core ^ flip), place_of(x, y, z, core))
        for x in range(SIDE)
        for y in range(SIDE)
        for z in range(SIDE)
        for core in range(CORES)
    ]


def fetch(values, **offset):
    return lax.ppermute(values, BOTH, from_offset(**offset))


def nt(a, b):
    return lax.dot_general(a, b, (((1,), (1,)), ((), ())), preferred_element_type=F32)


def nn(a, b):
    return lax.dot_general(a, b, (((1,), (0,)), ((), ())), preferred_element_type=F32)


def tn(a, b):
    return lax.dot_general(a, b, (((0,), (0,)), ((), ())), preferred_element_type=F32)


def row_sum(v):
    return jnp.sum(v, axis=1, keepdims=True)


def send_kernel(items, count, conf, out):
    def one(t, carry):
        tile = conf[t]
        tile = jnp.where(t < count[0], tile, jnp.zeros_like(tile))
        out[items[t]] = tile.T
        return carry

    lax.fori_loop(0, TILES, one, 0, unroll=4)


def send_conf_of(items, count, conf):
    smem = pl.BlockSpec(memory_space=pltpu.SMEM)
    vmem = pl.BlockSpec(memory_space=pltpu.VMEM)
    return pl.pallas_call(
        send_kernel,
        out_shape=jax.ShapeDtypeStruct((TILES, BS, BS), BF),
        in_specs=[smem, smem, vmem],
        out_specs=vmem,
        compiler_params=pltpu.CompilerParams(vmem_limit_bytes=VMEM_BYTES),
        cost_estimate=pl.CostEstimate(flops=0, bytes_accessed=16_000_000, transcendentals=0),
        name="send_conf",
    )(items, count, conf)


def user_kernel(
    items, users, count, gram_here, gram_there, conf_hbm, *rest,
):
    pieces, rest = rest[:16], rest[16:]
    (
        out, rows_hbm, gram_out,
        conf, factors, tails, exposure, slots, heads, gram, right, direction, narrow, mapped, answer, residual, sems,
    ) = rest
    conf_copy = pltpu.make_async_copy(conf_hbm, conf.at[pl.ds(0, TILES)], sems.at[0])
    panel = lax.axis_index("blk")
    core = lax.rem(lax.axis_index("grp"), CORES)
    here = (lax.div(panel, XLO * SIDE), lax.rem(lax.div(panel, SIDE), XLO), lax.rem(panel, SIDE))
    n = 0
    for kind in range(2):
        for flip in range(CORES):
            for outer in OFFSETS:
                for j, inner in enumerate(OFFSETS):
                    dy, dz = (inner, outer) if kind == 0 else (outer, inner)
                    y = lax.rem(here[0] + dy + SIDE, SIDE)
                    z = lax.rem(here[2] + dz + SIDE, SIDE)
                    for k in range(XLO):
                        x = here[1] if k == 0 else 1 - here[1]
                        half = ((y * XLO + x) * SIDE + z) * 2 + (core if flip == 0 else 1 - core)
                        source = pieces[n].at[j * XLO + k]
                        first = half * HALF + (0 if kind == 0 else PART_A)
                        size = PART_A if kind == 0 else PART_B
                        pltpu.make_async_copy(
                            source.at[pl.ds(0, size)],
                            factors.at[pl.ds(pl.multiple_of(first, 16), size)],
                            sems.at[1],
                        ).start()
                        if kind == 0:
                            pltpu.make_async_copy(
                                source.at[pl.ds(PART_A, TAIL)], tails.at[half], sems.at[3]
                            ).start()
                n += 1
    conf_copy.start()
    conf[TILES] = jnp.zeros((BS, BS), BF)
    live = count[0]

    for b in range(UB):
        heads[b] = 0

    def tally(t, carry):
        b = users[t]
        heads[b] = heads[b] + 1
        return carry

    lax.fori_loop(0, live, tally, 0)
    ends = []
    begin = jnp.int32(0)
    for b in range(UB):
        size = heads[b]
        heads[b] = begin
        begin = begin + (size + GROUP - 1) // GROUP * GROUP
        ends.append(begin)
    batches = (ends[-1] + GROUP * BATCH - 1) // (GROUP * BATCH)

    def blank(s, carry):
        slots[s] = TILES
        return carry

    lax.fori_loop(0, batches * (GROUP * BATCH), blank, 0)

    def place(t, carry):
        b = users[t]
        s = heads[b]
        slots[s] = t
        heads[b] = s + 1
        return carry

    lax.fori_loop(0, live, place, 0)

    pltpu.make_async_copy(factors, factors, sems.at[1]).wait()
    pltpu.make_async_copy(tails, tails, sems.at[3]).wait()

    def level_step(h, carry):
        row = tails[h].astype(F32)[0:1, :]
        exposure[pl.ds(2 * h, 1), :] = row[:, :BS]
        exposure[pl.ds(2 * h + 1, 1), :] = row[:, BS:]
        return carry

    lax.fori_loop(0, TILES // 2, level_step, 0, unroll=8)

    gram[...] = gram_here[...] + gram_there[...]
    conf_copy.wait()

    def group_of(g):
        first = g * GROUP
        b = (
            (first >= ends[0]).astype(jnp.int32)
            + (first >= ends[1]).astype(jnp.int32)
            + (first >= ends[2]).astype(jnp.int32)
        )
        confs, parts, levels = [], [], []
        for j in range(GROUP):
            t = slots[first + j]
            item = items[jnp.minimum(t, TILES - 1)]
            confs.append(conf[t])
            parts.append(factors[pl.ds(pl.multiple_of(item * BS, BS), BS), :])
            levels.append(exposure[pl.ds(item, 1), :])
        rows = pl.ds(pl.multiple_of(b * BS, BS), BS)
        return rows, jnp.concatenate(confs, axis=1), jnp.concatenate(parts, axis=0), levels

    right[...] = jnp.zeros_like(right)

    def right_step(g):
        rows, weights, parts, _ = group_of(g)
        right[rows, :] += nn(weights, parts)

    def each_group(step):
        def batch(n, carry):
            for j in range(BATCH):
                step(n * BATCH + j)
            return carry

        lax.fori_loop(0, batches, batch, 0)

    each_group(right_step)

    def map_step(g):
        rows, weights, parts, levels = group_of(g)
        wide = weights.astype(F32)
        excess = jnp.where(wide > 0, wide - jnp.concatenate(levels, axis=1), 0.0)
        scores = nt(narrow[rows, :], parts)
        mapped[rows, :] += nn((excess * scores).astype(BF), parts)

    residual[...] = right[...]
    direction[...] = right[...]
    answer[...] = jnp.zeros_like(answer)
    norm = row_sum(right[...] * right[...])
    for step in range(STEPS):
        way = direction[...]
        narrow[...] = way.astype(BF)
        mapped[...] = way + jnp.dot(way, gram[...], precision=HIGH, preferred_element_type=F32)
        each_group(map_step)
        image = mapped[...]
        stride = norm / row_sum(way * image)
        answer[...] += stride * way
        if step < STEPS - 1:
            rest = residual[...] - stride * image
            residual[...] = rest
            norm_next = row_sum(rest * rest)
            direction[...] = rest + norm_next / norm * way
            norm = norm_next

    result = answer[...].astype(BF)
    out[...] = result

    def send_row(t, carry):
        rows = pl.ds(pl.multiple_of(users[t] * BS, BS), BS)
        pltpu.make_async_copy(out.at[rows, :], rows_hbm.at[items[t]], sems.at[2]).start()
        return carry

    lax.fori_loop(0, TILES, send_row, 0)
    gram_out[...] = tn(result, result)
    pltpu.make_async_copy(rows_hbm, rows_hbm, sems.at[2]).wait()


def gram_kernel(*refs):
    parts_a, parts_b, out = refs[:SIDE], refs[SIDE : 2 * SIDE], refs[-1]
    out[...] = jnp.zeros_like(out)
    for n in range(SIDE):
        for m in range(SIDE):
            for k in range(XLO):
                first = parts_a[n][m * XLO + k]
                rows = jnp.concatenate([first[:PART_A], parts_b[m][n * XLO + k]], axis=0)
                weights = first[PART_A:].astype(F32)[0:1, :]
                scaled = rows.astype(F32).T * weights
                high = scaled.astype(BF)
                low = (scaled - high.astype(F32)).astype(BF)
                out[...] += nn(high, rows) + nn(low, rows)


def gram_half(parts_a, parts_b):
    vmem = pl.BlockSpec(memory_space=pltpu.VMEM)
    return pl.pallas_call(
        gram_kernel,
        out_shape=jax.ShapeDtypeStruct((RANK, RANK), F32),
        in_specs=[vmem] * (2 * SIDE),
        out_specs=vmem,
        compiler_params=pltpu.CompilerParams(vmem_limit_bytes=VMEM_BYTES),
        cost_estimate=pl.CostEstimate(flops=1_000_000_000, bytes_accessed=1_000_000, transcendentals=0),
        name="gram_half",
    )(*parts_a, *parts_b)


def user_half(items, users, count, grams, conf, pieces):
    smem = pl.BlockSpec(memory_space=pltpu.SMEM)
    vmem = pl.BlockSpec(memory_space=pltpu.VMEM)
    far = pl.BlockSpec(memory_space=pl.ANY)
    wide = pltpu.VMEM((UB * BS, RANK), F32)
    return pl.pallas_call(
        user_kernel,
        out_shape=(
            jax.ShapeDtypeStruct((UB * BS, RANK), BF),
            jax.ShapeDtypeStruct((TILES, BS, RANK), BF),
            jax.ShapeDtypeStruct((RANK, RANK), F32),
        ),
        in_specs=[smem, smem, smem, vmem, vmem, far] + [far] * len(pieces),
        out_specs=(vmem, far, vmem),
        scratch_shapes=[
            pltpu.VMEM((TILES + 1, BS, BS), BF),
            pltpu.VMEM((TILES * BS, RANK), BF),
            pltpu.VMEM((TILES // 2, TAIL, RANK), BF),
            pltpu.VMEM((TILES, BS), F32),
            pltpu.SMEM((SLOTS,), jnp.int32),
            pltpu.SMEM((UB,), jnp.int32),
            pltpu.VMEM((RANK, RANK), F32),
            wide,
            wide,
            pltpu.VMEM((UB * BS, RANK), BF),
            wide,
            wide,
            wide,
            pltpu.SemaphoreType.DMA((4,)),
        ],
        compiler_params=pltpu.CompilerParams(vmem_limit_bytes=VMEM_BYTES),
        cost_estimate=pl.CostEstimate(flops=5_000_000_000, bytes_accessed=4_000_000, transcendentals=0),
        name="user_half",
    )(items, users, count, *grams, conf, *pieces)


ITEM_GROUP = 16
CHUNKS = TILES // ITEM_GROUP


def item_tools(conf_hbm, rows_hbm, exposure, conf, rows, sems):
    def copies_of(c):
        part = pl.ds(c * ITEM_GROUP, ITEM_GROUP)
        return (
            pltpu.make_async_copy(rows_hbm.at[part], rows.at[part], sems.at[0, c]),
            pltpu.make_async_copy(conf_hbm.at[part], conf.at[part], sems.at[1, c]),
        )

    for c in range(CHUNKS):
        for copy in copies_of(c):
            copy.start()
    level = jnp.broadcast_to(exposure[...], (BS, BS)).T

    def chunk_of(c, waits):
        if waits:
            for copy in copies_of(c):
                copy.wait()
        weights = jnp.concatenate([conf[c * ITEM_GROUP + j] for j in range(ITEM_GROUP)], axis=1)
        part = rows[pl.ds(c * ITEM_GROUP, ITEM_GROUP)].reshape(ITEM_GROUP * BS, RANK)
        return weights, part

    def add_right(target):
        def step(c, carry):
            weights, part = chunk_of(c, True)
            target[...] += nn(weights, part)
            return carry

        lax.fori_loop(0, CHUNKS, step, 0, unroll=2)

    def add_returned(target, narrow, waits=False):
        level_wide = jnp.concatenate([level] * ITEM_GROUP, axis=1)

        def step(c, carry):
            weights, part = chunk_of(c, waits)
            wide = weights.astype(F32)
            excess = jnp.where(wide > 0, wide - level_wide, 0.0)
            scores = nt(narrow[...], part)
            target[...] += nn((excess * scores).astype(BF), part)
            return carry

        lax.fori_loop(0, CHUNKS, step, 0, unroll=2)

    return level, add_right, add_returned


def right_kernel(conf_hbm, rows_hbm, exposure, right, returned, conf, rows, narrow, sems):
    _, add_right, add_returned = item_tools(conf_hbm, rows_hbm, exposure, conf, rows, sems)
    right[...] = jnp.zeros_like(right)
    add_right(right)
    narrow[...] = right[...].astype(BF)
    returned[...] = jnp.zeros_like(returned)
    add_returned(returned, narrow)


def item_kernel(
    conf_hbm, rows_hbm, exposure, user_gram, right, returned, out, conf, rows, narrow, mapped, sems
):
    level, _, add_returned = item_tools(conf_hbm, rows_hbm, exposure, conf, rows, sems)
    level_rank = jnp.concatenate([level] * (RANK // BS), axis=1)
    residual = right[...]
    way = residual
    answer = jnp.zeros_like(residual)
    norm = row_sum(residual * residual)
    for step in range(STEPS):
        term = jnp.dot(way, user_gram[...], precision=HIGH, preferred_element_type=F32)
        mapped[...] = way + level_rank * term
        if step == 0:
            mapped[...] += returned[...]
        else:
            narrow[...] = way.astype(BF)
            add_returned(mapped, narrow, step == 1)
        image = mapped[...]
        stride = norm / row_sum(way * image)
        answer = answer + stride * way
        if step < STEPS - 1:
            residual = residual - stride * image
            norm_next = row_sum(residual * residual)
            way = residual + norm_next / norm * way
            norm = norm_next
    out[...] = (answer * (float(TILES) ** 0.5)).astype(BF)


def item_call(kernel, name, outs, scratch, conf, rows, *small):
    vmem = pl.BlockSpec(memory_space=pltpu.VMEM)
    far = pl.BlockSpec(memory_space=pl.ANY)
    return pl.pallas_call(
        kernel,
        out_shape=outs,
        in_specs=[far, far] + [vmem] * len(small),
        out_specs=[vmem] * len(outs),
        scratch_shapes=[
            pltpu.VMEM((TILES, BS, BS), BF),
            pltpu.VMEM((TILES, BS, RANK), BF),
            pltpu.VMEM((BS, RANK), BF),
            *scratch,
            pltpu.SemaphoreType.DMA((2, CHUNKS)),
        ],
        compiler_params=pltpu.CompilerParams(vmem_limit_bytes=VMEM_BYTES),
        cost_estimate=pl.CostEstimate(flops=12_000_000_000, bytes_accessed=13_000_000, transcendentals=0),
        name=name,
    )(conf, rows, *small)


def item_start(conf, rows, exposure):
    wide = jax.ShapeDtypeStruct((BS, RANK), F32)
    return item_call(right_kernel, "item_start", [wide, wide], [], conf, rows, exposure)


def item_half(conf, rows, exposure, user_gram, right, returned):
    out = jax.ShapeDtypeStruct((BS, RANK), BF)
    scratch = [pltpu.VMEM((BS, RANK), F32)]
    return item_call(
        item_kernel, "item_half", [out], scratch, conf, rows, exposure, user_gram, right, returned
    )[0]


def exchange(values, axes):
    return lax.all_to_all(values, axes, split_axis=0, concat_axis=0, tiled=True)


def sum_lines(values, core):
    rows = values.shape[0] // CORES
    first = values[:rows]
    second = values[rows:]
    half = jnp.where(core == 0, first, second) + fetch(jnp.where(core == 0, second, first), flip=1)
    return sum_axis(sum_axis(half, "dx"), "dy")


def sum_axis(half, axis):
    near, far, across = (fetch(half, **{axis: d}) for d in OFFSETS[1:])
    return (half + across) + (near + far)


def sum_rest(half, core):
    half = sum_axis(half, "dz")
    other = fetch(half, flip=1)
    return jnp.concatenate(
        [jnp.where(core == 0, half, other), jnp.where(core == 0, other, half)], axis=0
    )


def body(item_factors, exposure, confidence, tile_items, tile_users, tile_count):
    conf_tiles = confidence[0]
    items = tile_items[0]
    users = tile_users[0]
    core = lax.rem(lax.axis_index("grp"), CORES)
    mine = lax.dynamic_slice_in_dim(item_factors, core * HALF, HALF)
    tail = jnp.pad(
        lax.dynamic_slice_in_dim(exposure, core * HALF, HALF)[None], ((0, TAIL - 1), (0, 0))
    )
    part_a = jnp.concatenate([mine[:PART_A], tail], axis=0)
    part_b = mine[PART_A:]
    part_a = jnp.stack([part_a, fetch(part_a, dx=1)])
    part_b = jnp.stack([part_b, fetch(part_b, dx=-1)])
    line_a = jnp.concatenate([part_a] + [fetch(part_a, dy=d) for d in OFFSETS[1:]], axis=0)
    line_b = jnp.concatenate([part_b] + [fetch(part_b, dz=d) for d in OFFSETS[1:]], axis=0)
    send_conf = send_conf_of(items, tile_count, conf_tiles)
    full_a = [line_a] + [fetch(line_a, dz=d) for d in OFFSETS[1:]]
    full_b = [line_b] + [fetch(line_b, dy=d) for d in OFFSETS[1:]]
    full_a[1:], full_b[1:], send_conf = lax.optimization_barrier(
        (full_a[1:], full_b[1:], send_conf)
    )
    got_conf = exchange(send_conf, BOTH)
    pieces = (
        full_a + [fetch(v, flip=1) for v in full_a]
        + full_b + [fetch(v, flip=1) for v in full_b]
    )
    gram_own = gram_half(full_a, full_b)
    user_factors, send_rows, local_gram = user_half(
        items, users, tile_count, (gram_own, fetch(gram_own, flip=1)), conf_tiles, pieces
    )
    got_rows = exchange(send_rows, BOTH)
    half_gram = sum_lines(local_gram, core)
    own = lax.dynamic_slice_in_dim(exposure, lax.axis_index("grp") * BS, BS)
    own = own.astype(F32).reshape(1, BS)
    right, returned = item_start(got_conf, got_rows, own)
    half_gram, right, returned = lax.optimization_barrier((half_gram, right, returned))
    user_gram = sum_rest(half_gram, core) * (1.0 / (UB * BS))
    item_update = item_half(got_conf, got_rows, own, user_gram, right, returned)
    return user_factors, item_update, user_gram


def solution(mesh):
    placed = (
        P("blk", None),
        P("blk"),
        P(BOTH, None, None, None),
        P(BOTH, None),
        P(BOTH, None),
        P(BOTH),
    )
    return jax.shard_map(
        body,
        mesh=mesh,
        in_specs=placed,
        out_specs=(P(BOTH, None), P(BOTH, None), P()),
        check_vma=False,
    )
```

time: 462 us -> 288 us (0.62)
  waiting for transfers between devices: 281 us -> 153 us
  Pallas kernels: 82.9 us -> 60.6 us
  blocking collectives: 15.9 us -> 0 us
  local copies, waits for them, and re-layouts: 15.5 us -> 4.78 us
  starting transfers between devices: 54.3 us -> 62.3 us
    all_to_all x4 -> x2, waiting for transfers between devices: 281 us -> 15 us  [exchange(): return lax.all_to_all(values, axes, split_axis=0, concat_axis=0, tiled=True)]
    ppermute x0 -> x34, waiting for transfers between devices: none -> 138 us  [fetch(): return lax.ppermute(values, BOTH, from_offset(**offset))]
    ppermute x0 -> x34, starting transfers between devices: none -> 43.7 us  [fetch(): return lax.ppermute(values, BOTH, from_offset(**offset))]
    all_to_all x4 -> x2, starting transfers between devices: 54.3 us -> 18.6 us  [exchange(): return lax.all_to_all(values, axes, split_axis=0, concat_axis=0, tiled=True)]
    pallas_call x1, Pallas kernels: 44.3 us -> 22.8 us  [user_half(): pl.pallas_call(user_kernel, out_shape=(jax.ShapeDtypeStruct((UB * BS, RAN...]
    all_to_all x1 -> x0, blocking collectives: 15.9 us -> none  [exchange(): return lax.all_to_all(values, axes, split_axis=0, concat_axis=0, tiled=True)]
    slice x1, local copies, waits for them, and re-layouts: 7.48 us -> 0.82 us  [body(): part_a = jnp.concatenate([mine[:PART_A], tail], axis=0)]
    pallas_call x1 -> x3, Pallas kernels: 31.4 us -> 30.4 us  [the longest x2 24.7 us: item_call(): pl.pallas_call(kernel, out_shape=outs, in_specs=[far, far] + [vmem] * len...]
  transfers between devices with their start and end apart: 4 -> 36, of which waited for: 4 -> 17; matrix products, arithmetic and copies ran while one was open for 0% -> 1% of each run, Pallas kernels for 2% -> 13%
where the time goes in v2:
time: 288 us; the launch traced here: 284 us
  waiting for transfers between devices  153 us (53%)
  starting transfers between devices  62.3 us (22%)
  Pallas kernels  60.6 us (21%)
  local copies, waits for them, and re-layouts  4.78 us (2%)
    ppermute x34, waiting for transfers between devices, fetch(): return lax.ppermute(values, BOTH, from_offset(**offset))  138 us
    ppermute x34, starting transfers between devices, fetch(): return lax.ppermute(values, BOTH, from_offset(**offset))  43.7 us
    pallas_call x2, Pallas kernels, item_call(): pl.pallas_call(kernel, out_shape=outs, in_specs=[far, far] + [vmem] * len...  24.7 us
    pallas_call x1, Pallas kernels, user_half(): pl.pallas_call(user_kernel, out_shape=(jax.ShapeDtypeStruct((UB * BS, RAN...  22.8 us
    all_to_all x2, starting transfers between devices, exchange(): return lax.all_to_all(values, axes, split_axis=0, concat_axis=0, tiled=True)  18.6 us
    all_to_all x2, waiting for transfers between devices, exchange(): return lax.all_to_all(values, axes, split_axis=0, concat_axis=0, tiled=True)  15 us
    pallas_call x1, Pallas kernels, send_conf_of(): pl.pallas_call(send_kernel, out_shape=jax.ShapeDtypeStruct((TILES, BS, BS...  7.4 us
  transfers between devices with their start and end apart: 36, of which 17 were waited for; matrix products, arithmetic and copies ran while one was open for 1% of the time, Pallas kernels for 13%

profile of v2, /device:TPU:15, one launch (start us, length us, event | category | flops | bytes accessed | tf_op | source)
XLA Modules:
  0.0 283.9 jit_solution(5054946399463426951)
XLA Ops:
  0.6 0.8 dynamic_slice.10
  1.4 0.8 constant_dynamic-slice_fusion
  2.2 0.6 collective-permute-start
  2.9 0.9 constant_dynamic-update-slice_fusion.9
  3.8 2.2 collective-permute-start.7
  6.0 0.7 collective-permute-done
  6.7 2.1 collective-permute-start.3
  8.8 1.5 collective-permute-start.1
  10.3 3.7 %collective-permute-start.10 = (bf16[2,144,256]{2,1,0:T(8,128)(2,1)S(1)}, bf16[2,144,256]{2,1,0:T(8,128)(2,1)S(1)}, u32[]{:S(2)}, u32[]{:S(2)}) collective-permute-start(bf16[2,144,256]{2,1,0:T(8,128)(2,1)S(1)} %pad_maximum_fusion), channel_id=1, source_target_pairs={{8,0},{9,1},{12,4},{13,5},{0,8},{1,9},{4,12},{5,13},{40,32},{41,33... | collective-permute-start | bytes 442376 | tf_op jit(solution)/shard_map/ppermute | solution.py:49
  13.9 0.7 collective-permute-start.9
  14.7 3.6 %collective-permute-start.8 = (bf16[2,144,256]{2,1,0:T(8,128)(2,1)S(1)}, bf16[2,144,256]{2,1,0:T(8,128)(2,1)S(1)}, u32[]{:S(2)}, u32[]{:S(2)}) collective-permute-start(bf16[2,144,256]{2,1,0:T(8,128)(2,1)S(1)} %pad_maximum_fusion), channel_id=1, source_target_pairs={{4,0},{5,1},{8,4},{9,5},{12,8},{13,9},{0,12},{1,13},{36,32},{37,33... | collective-permute-start | bytes 442376 | tf_op jit(solution)/shard_map/ppermute | solution.py:49
  18.5 14.5 %collective-permute-done.8 = bf16[2,144,256]{2,1,0:T(8,128)(2,1)S(1)} collective-permute-done((bf16[2,144,256]{2,1,0:T(8,128)(2,1)S(1)}, bf16[2,144,256]{2,1,0:T(8,128)(2,1)S(1)}, u32[]{:S(2)}, u32[]{:S(2)}) %collective-permute-start.8) | collective-permute-done | bytes 147488 | tf_op jit(solution)/shard_map/ppermute | solution.py:49
  33.2 3.4 %collective-permute-start.12 = (bf16[8,144,256]{2,1,0:T(8,128)(2,1)S(1)}, bf16[8,144,256]{2,1,0:T(8,128)(2,1)S(1)}, u32[]{:S(2)}, u32[]{:S(2)}) collective-permute-start(bf16[8,144,256]{2,1,0:T(8,128)(2,1)S(1)} %constant_dynamic-update-slice_fusion.5.refs_4_.rest_8_), channel_id=1, source_target_pairs={{96,0},{97,1},{100,4},{101,5},{104,8},{105,9},{108,12},{109,13},{0... | collective-permute-start | bytes 1769480 | tf_op jit(solution)/shard_map/ppermute | solution.py:49
  36.6 3.6 %collective-permute-start.4 = (bf16[8,128,256]{2,1,0:T(8,128)(2,1)S(1)}, bf16[8,128,256]{2,1,0:T(8,128)(2,1)S(1)}, u32[]{:S(2)}, u32[]{:S(2)}) collective-permute-start(bf16[8,128,256]{2,1,0:T(8,128)(2,1)S(1)} %constant_dynamic-update-slice_fusion.refs_0_.rest_0_), channel_id=1, source_target_pairs={{4,0},{5,1},{8,4},{9,5},{12,8},{13,9},{0,12},{1,13},{36,32},{37,33... | collective-permute-start | bytes 1572872 | tf_op jit(solution)/shard_map/ppermute | solution.py:49
  40.8 7.4 %send_conf.1 = bf16[128,128,128]{2,1,0:T(8,128)(2,1)} custom-call(s32[128]{0:T(128)} %bitcast.20, s32[1]{0:T(128)S(6)} %copy.17.count, bf16[128,128,128]{2,1,0:T(8,128)(2,1)} %bitcast.15), custom_call_target="tpu_custom_call" | custom-call | bytes 16000000 | tf_op jit(solution)/shard_map/send_conf/pallas_call | solution.py:81
  48.2 1.3 collective-permute-done.5.refs_2_.rest_2_
  49.6 11.2 %collective-permute-done.12.refs_6_.rest_10_ = bf16[8,144,256]{2,1,0:T(8,128)(2,1)S(1)} collective-permute-done((bf16[8,144,256]{2,1,0:T(8,128)(2,1)S(1)}, bf16[8,144,256]{2,1,0:T(8,128)(2,1)S(1)}, u32[]{:S(2)}, u32[]{:S(2)}) %collective-permute-start.12) | collective-permute-done | bytes 589856 | tf_op jit(solution)/shard_map/ppermute | solution.py:49
  60.8 1.8 collective-permute-done.11.refs_5_.rest_9_
  62.5 0.8 copy-done.7
  63.3 10.2 %all-to-all-start = ((bf16[128,128,128]{2,1,0:T(8,128)(2,1)}), bf16[128,128,128]{2,1,0:T(8,128)(2,1)}, u32[]{:S(2)}, u32[]{:S(2)}) async-start(bf16[128,128,128]{2,1,0:T(8,128)(2,1)} %send_conf.1), calls=%async_computation | async-start | bytes 8388608 | tf_op jit(solution)/shard_map/all_to_all | solution.py:436
  73.6 0.4 collective-permute-start.19
  74.5 5.7 %gram_half.1.gram_here = f32[256,256]{1,0:T(8,128)} custom-call(bf16[8,128,256]{2,1,0:T(8,128)(2,1)} %copy-done.2, bf16[8,128,256]{2,1,0:T(8,128)(2,1)} %copy-done.13, bf16[8,128,256]{2,1,0:T(8,128)(2,1)} %copy-done.11, bf16[8,128,256]{2,1,0:T(8,128)(2,1)} %copy-done.9, bf16[8,144,256]{2,1,0:T(8,128)(2,1)} %copy-done.1, bf16[8,144,256]{2,1,0:T(8,128)(2,1)} %copy-done.7, ...), custom_call_target="tpu_custom_call" | custom-call | flops 1000000000 | bytes 1000000 | tf_op jit(solution)/shard_map/gram_half/pallas_call | solution.py:268
  81.4 0.6 collective-permute-done.14.gram_there
  82.5 2.5 collective-permute-done.17.rest_6_
  85.0 0.7 collective-permute-done.18.rest_7_
  85.8 0.7 copy-done.22
  87.2 22.8 %user_half.1 = (bf16[512,256]{1,0:T(8,128)(2,1)}, bf16[128,128,256]{2,1,0:T(8,128)(2,1)}, f32[256,256]{1,0:T(8,128)}) custom-call(s32[128]{0:T(128)} %bitcast.21, s32[128]{0:T(128)} %bitcast.22, s32[1]{0:T(128)S(6)} %copy.17.count, f32[256,256]{1,0:T(8,128)} %gram_half.1.gram_here, f32[256,256]{1,0:T(8,128)} %copy-done.23, bf16[128,128,128]{2,1,0:T(8,128)(2,1)} %bitcast.16, ...), custom_call_target="tpu_custom_call" | custom-call | flops 5000000000 | bytes 4000000 | tf_op jit(solution)/shard_map/user_half/pallas_call | solution.py:284
  110.0 14.9 %all-to-all-done.conf_hbm = bf16[128,128,128]{2,1,0:T(8,128)(2,1)} async-done(((bf16[128,128,128]{2,1,0:T(8,128)(2,1)}), bf16[128,128,128]{2,1,0:T(8,128)(2,1)}, u32[]{:S(2)}, u32[]{:S(2)}) %all-to-all-start) | async-done | bytes 4194336 | tf_op jit(solution)/shard_map/all_to_all | solution.py:436
  124.9 8.5 %all-to-all-start.1 = ((bf16[128,128,256]{2,1,0:T(8,128)(2,1)}), bf16[128,128,256]{2,1,0:T(8,128)(2,1)}, u32[]{:S(2)}, u32[]{:S(2)}) async-start(bf16[128,128,256]{2,1,0:T(8,128)(2,1)} %get-tuple-element.26), calls=%async_computation.1 | async-start | bytes 16777216 | tf_op jit(solution)/shard_map/all_to_all | solution.py:436
  133.9 1.0 collective-permute-done.23
  135.2 1.2 collective-permute-start.25
  136.4 1.2 collective-permute-start.24
  137.6 93.1 %collective-permute-done.26 = f32[128,256]{1,0:T(8,128)S(1)} collective-permute-done((f32[128,256]{1,0:T(8,128)S(1)}, f32[128,256]{1,0:T(8,128)S(1)}, u32[]{:S(2)}, u32[]{:S(2)}) %collective-permute-start.26) | collective-permute-done | bytes 131104 | tf_op jit(solution)/shard_map/ppermute | solution.py:49
  230.7 2.2 collective-permute-done.24
  233.0 1.5 collective-permute-start.28
  234.4 2.5 collective-permute-start.27
  236.9 0.6 bitcast_convert_fusion.exposure
  237.5 0.9 collective-permute-done.28
  238.4 2.9 %collective-permute-done.27 = f32[128,256]{1,0:T(8,128)S(1)} collective-permute-done((f32[128,256]{1,0:T(8,128)S(1)}, f32[128,256]{1,0:T(8,128)S(1)}, u32[]{:S(2)}, u32[]{:S(2)}) %collective-permute-start.27) | collective-permute-done | bytes 131104 | tf_op jit(solution)/shard_map/ppermute | solution.py:49
  241.4 11.1 %item_start.1 = (f32[128,256]{1,0:T(8,128)}, f32[128,256]{1,0:T(8,128)}) custom-call(bf16[128,128,128]{2,1,0:T(8,128)(2,1)} %all-to-all-done.conf_hbm, bf16[128,128,256]{2,1,0:T(8,128)(2,1)} %all-to-all-done.1.rows_hbm, f32[1,128]{1,0:T(1,128)} %bitcast_convert_fusion.exposure), custom_call_target="tpu_custom_call" | custom-call | flops 12000000000 | bytes 13000000 | tf_op jit(solution)/shard_map/item_start/pallas_call | solution.py:404
  252.4 6.7 %collective-permute-start.32 = (f32[128,256]{1,0:T(8,128)S(1)}, f32[128,256]{1,0:T(8,128)S(1)}, u32[]{:S(2)}, u32[]{:S(2)}) collective-permute-start(f32[128,256]{1,0:T(8,128)S(1)} %add_add_fusion.1), channel_id=1, source_target_pairs={{12,0},{13,1},{0,4},{1,5},{4,8},{5,9},{8,12},{9,13},{44,32},{45,33... | collective-permute-start | bytes 393224 | tf_op jit(solution)/shard_map/ppermute | solution.py:49
  259.2 2.8 collective-permute-start.30
  261.9 1.0 collective-permute-done.31
  263.0 2.6 collective-permute-done.30
  265.6 2.7 collective-permute-start.33
  268.3 1.0 collective-permute-done.33
  269.3 0.7 maximum_multiply_fusion.user_gram
  270.0 13.7 %item_half.1 = bf16[128,256]{1,0:T(8,128)(2,1)} custom-call(bf16[128,128,128]{2,1,0:T(8,128)(2,1)} %all-to-all-done.conf_hbm, bf16[128,128,256]{2,1,0:T(8,128)(2,1)} %all-to-all-done.1.rows_hbm, f32[1,128]{1,0:T(1,128)} %bitcast_convert_fusion.exposure, f32[256,256]{1,0:T(8,128)} %maximum_multiply_fusion.user_gram, f32[128,256]{1,0:T(8,128)} %get-tuple-element.31.right, ...), custom_call_target="tpu_custom_call" | custom-call | flops 12000000000 | bytes 13000000 | tf_op jit(solution)/shard_map/item_half/pallas_call | solution.py:404
  (103 shorter events, 4.4 us)
Async XLA Ops:
  2.2 4.4 %collective-permute-start = (bf16[128,256]{1,0:T(8,128)(2,1)S(1)}, bf16[128,256]{1,0:T(8,128)(2,1)S(1)}, u32[]{:S(2)}, u32[]{:S(2)}) collective-permute-start(bf16[128,256]{1,0:T(8,128)(2,1)S(1)} %get-tuple-element.38), channel_id=1, source_target_pairs={{16,0},{17,1},{20,4},{21,5},{24,8},{25,9},{28,12},{29,13},{48,32},... | collective-permute-start | bytes 196616 | tf_op jit(solution)/shard_map/ppermute | solution.py:49
  3.8 6.5 %collective-permute-start.7 = (bf16[144,256]{1,0:T(8,128)(2,1)S(1)}, bf16[144,256]{1,0:T(8,128)(2,1)S(1)}, u32[]{:S(2)}, u32[]{:S(2)}) collective-permute-start(bf16[144,256]{1,0:T(8,128)(2,1)S(1)} %get-tuple-element.34), channel_id=1, source_target_pairs={{18,0},{19,1},{22,4},{23,5},{26,8},{27,9},{30,12},{31,13},{50,32},... | collective-permute-start | bytes 221192 | tf_op jit(solution)/shard_map/ppermute | solution.py:49
  6.7 11.7 %collective-permute-start.3 = (bf16[2,128,256]{2,1,0:T(8,128)(2,1)S(1)}, bf16[2,128,256]{2,1,0:T(8,128)(2,1)S(1)}, u32[]{:S(2)}, u32[]{:S(2)}) collective-permute-start(bf16[2,128,256]{2,1,0:T(8,128)(2,1)S(1)} %pad_maximum_fusion.1), channel_id=1, source_target_pairs={{64,0},{65,1},{68,4},{69,5},{72,8},{73,9},{76,12},{77,13},{96,32},... | collective-permute-start | bytes 393224 | tf_op jit(solution)/shard_map/ppermute | solution.py:49
  8.7 9.6 %collective-permute-start.2 = (bf16[2,128,256]{2,1,0:T(8,128)(2,1)S(1)}, bf16[2,128,256]{2,1,0:T(8,128)(2,1)S(1)}, u32[]{:S(2)}, u32[]{:S(2)}) collective-permute-start(bf16[2,128,256]{2,1,0:T(8,128)(2,1)S(1)} %pad_maximum_fusion.1), channel_id=1, source_target_pairs={{96,0},{97,1},{100,4},{101,5},{104,8},{105,9},{108,12},{109,13},{0... | collective-permute-start | bytes 393224 | tf_op jit(solution)/shard_map/ppermute | solution.py:49
  8.8 5.9 %collective-permute-start.1 = (bf16[2,128,256]{2,1,0:T(8,128)(2,1)S(1)}, bf16[2,128,256]{2,1,0:T(8,128)(2,1)S(1)}, u32[]{:S(2)}, u32[]{:S(2)}) collective-permute-start(bf16[2,128,256]{2,1,0:T(8,128)(2,1)S(1)} %pad_maximum_fusion.1), channel_id=1, source_target_pairs={{32,0},{33,1},{36,4},{37,5},{40,8},{41,9},{44,12},{45,13},{64,32},... | collective-permute-start | bytes 393224 | tf_op jit(solution)/shard_map/ppermute | solution.py:49
  10.3 22.8 %collective-permute-start.10 = (bf16[2,144,256]{2,1,0:T(8,128)(2,1)S(1)}, bf16[2,144,256]{2,1,0:T(8,128)(2,1)S(1)}, u32[]{:S(2)}, u32[]{:S(2)}) collective-permute-start(bf16[2,144,256]{2,1,0:T(8,128)(2,1)S(1)} %pad_maximum_fusion), channel_id=1, source_target_pairs={{8,0},{9,1},{12,4},{13,5},{0,8},{1,9},{4,12},{5,13},{40,32},{41,33... | collective-permute-start | bytes 442376 | tf_op jit(solution)/shard_map/ppermute | solution.py:49
  13.9 19.1 %collective-permute-start.9 = (bf16[2,144,256]{2,1,0:T(8,128)(2,1)S(1)}, bf16[2,144,256]{2,1,0:T(8,128)(2,1)S(1)}, u32[]{:S(2)}, u32[]{:S(2)}) collective-permute-start(bf16[2,144,256]{2,1,0:T(8,128)(2,1)S(1)} %pad_maximum_fusion), channel_id=1, source_target_pairs={{12,0},{13,1},{0,4},{1,5},{4,8},{5,9},{8,12},{9,13},{44,32},{45,33... | collective-permute-start | bytes 442376 | tf_op jit(solution)/shard_map/ppermute | solution.py:49
  14.7 18.3 %collective-permute-start.8 = (bf16[2,144,256]{2,1,0:T(8,128)(2,1)S(1)}, bf16[2,144,256]{2,1,0:T(8,128)(2,1)S(1)}, u32[]{:S(2)}, u32[]{:S(2)}) collective-permute-start(bf16[2,144,256]{2,1,0:T(8,128)(2,1)S(1)} %pad_maximum_fusion), channel_id=1, source_target_pairs={{4,0},{5,1},{8,4},{9,5},{12,8},{13,9},{0,12},{1,13},{36,32},{37,33... | collective-permute-start | bytes 442376 | tf_op jit(solution)/shard_map/ppermute | solution.py:49
  18.4 55.6 %copy-start.2 = (bf16[8,128,256]{2,1,0:T(8,128)(2,1)}, bf16[8,128,256]{2,1,0:T(8,128)(2,1)S(1)}, u32[]{:S(2)}) copy-start(bf16[8,128,256]{2,1,0:T(8,128)(2,1)S(1)} %constant_dynamic-update-slice_fusion.refs_0_.rest_0_) | copy-start | bytes 1572868
  18.4 18.1 %collective-permute-start.6 = (bf16[8,128,256]{2,1,0:T(8,128)(2,1)S(1)}, bf16[8,128,256]{2,1,0:T(8,128)(2,1)S(1)}, u32[]{:S(2)}, u32[]{:S(2)}) collective-permute-start(bf16[8,128,256]{2,1,0:T(8,128)(2,1)S(1)} %constant_dynamic-update-slice_fusion.refs_0_.rest_0_), channel_id=1, source_target_pairs={{8,0},{9,1},{12,4},{13,5},{0,8},{1,9},{4,12},{5,13},{40,32},{41,33... | collective-permute-start | bytes 1572872 | tf_op jit(solution)/shard_map/ppermute | solution.py:49
  33.0 40.5 %copy-start.1 = (bf16[8,144,256]{2,1,0:T(8,128)(2,1)}, bf16[8,144,256]{2,1,0:T(8,128)(2,1)S(1)}, u32[]{:S(2)}) copy-start(bf16[8,144,256]{2,1,0:T(8,128)(2,1)S(1)} %constant_dynamic-update-slice_fusion.5.refs_4_.rest_8_) | copy-start | bytes 1769476
  33.1 16.5 %collective-permute-start.13 = (bf16[8,144,256]{2,1,0:T(8,128)(2,1)S(1)}, bf16[8,144,256]{2,1,0:T(8,128)(2,1)S(1)}, u32[]{:S(2)}, u32[]{:S(2)}) collective-permute-start(bf16[8,144,256]{2,1,0:T(8,128)(2,1)S(1)} %constant_dynamic-update-slice_fusion.5.refs_4_.rest_8_), channel_id=1, source_target_pairs={{64,0},{65,1},{68,4},{69,5},{72,8},{73,9},{76,12},{77,13},{96,32},... | collective-permute-start | bytes 1769480 | tf_op jit(solution)/shard_map/ppermute | solution.py:49
  33.2 27.6 %collective-permute-start.12 = (bf16[8,144,256]{2,1,0:T(8,128)(2,1)S(1)}, bf16[8,144,256]{2,1,0:T(8,128)(2,1)S(1)}, u32[]{:S(2)}, u32[]{:S(2)}) collective-permute-start(bf16[8,144,256]{2,1,0:T(8,128)(2,1)S(1)} %constant_dynamic-update-slice_fusion.5.refs_4_.rest_8_), channel_id=1, source_target_pairs={{96,0},{97,1},{100,4},{101,5},{104,8},{105,9},{108,12},{109,13},{0... | collective-permute-start | bytes 1769480 | tf_op jit(solution)/shard_map/ppermute | solution.py:49
  36.5 26.0 %collective-permute-start.11 = (bf16[8,144,256]{2,1,0:T(8,128)(2,1)S(1)}, bf16[8,144,256]{2,1,0:T(8,128)(2,1)S(1)}, u32[]{:S(2)}, u32[]{:S(2)}) collective-permute-start(bf16[8,144,256]{2,1,0:T(8,128)(2,1)S(1)} %constant_dynamic-update-slice_fusion.5.refs_4_.rest_8_), channel_id=1, source_target_pairs={{32,0},{33,1},{36,4},{37,5},{40,8},{41,9},{44,12},{45,13},{64,32},... | collective-permute-start | bytes 1769480 | tf_op jit(solution)/shard_map/ppermute | solution.py:49
  36.5 13.0 %collective-permute-start.5 = (bf16[8,128,256]{2,1,0:T(8,128)(2,1)S(1)}, bf16[8,128,256]{2,1,0:T(8,128)(2,1)S(1)}, u32[]{:S(2)}, u32[]{:S(2)}) collective-permute-start(bf16[8,128,256]{2,1,0:T(8,128)(2,1)S(1)} %constant_dynamic-update-slice_fusion.refs_0_.rest_0_), channel_id=1, source_target_pairs={{12,0},{13,1},{0,4},{1,5},{4,8},{5,9},{8,12},{9,13},{44,32},{45,33... | collective-permute-start | bytes 1572872 | tf_op jit(solution)/shard_map/ppermute | solution.py:49
  36.5 11.7 %copy-start.9 = (bf16[8,128,256]{2,1,0:T(8,128)(2,1)}, bf16[8,128,256]{2,1,0:T(8,128)(2,1)S(1)}, u32[]{:S(2)}) copy-start(bf16[8,128,256]{2,1,0:T(8,128)(2,1)S(1)} %collective-permute-done.6.refs_3_.rest_3_) | copy-start | bytes 1572868
  36.6 13.0 %collective-permute-start.4 = (bf16[8,128,256]{2,1,0:T(8,128)(2,1)S(1)}, bf16[8,128,256]{2,1,0:T(8,128)(2,1)S(1)}, u32[]{:S(2)}, u32[]{:S(2)}) collective-permute-start(bf16[8,128,256]{2,1,0:T(8,128)(2,1)S(1)} %constant_dynamic-update-slice_fusion.refs_0_.rest_0_), channel_id=1, source_target_pairs={{4,0},{5,1},{8,4},{9,5},{12,8},{13,9},{0,12},{1,13},{36,32},{37,33... | collective-permute-start | bytes 1572872 | tf_op jit(solution)/shard_map/ppermute | solution.py:49
  49.6 11.2 %copy-start.11 = (bf16[8,128,256]{2,1,0:T(8,128)(2,1)}, bf16[8,128,256]{2,1,0:T(8,128)(2,1)S(1)}, u32[]{:S(2)}) copy-start(bf16[8,128,256]{2,1,0:T(8,128)(2,1)S(1)} %collective-permute-done.5.refs_2_.rest_2_) | copy-start | bytes 1572868
  49.6 11.2 %copy-start.13 = (bf16[8,128,256]{2,1,0:T(8,128)(2,1)}, bf16[8,128,256]{2,1,0:T(8,128)(2,1)S(1)}, u32[]{:S(2)}) copy-start(bf16[8,128,256]{2,1,0:T(8,128)(2,1)S(1)} %collective-permute-done.4.refs_1_.rest_1_) | copy-start | bytes 1572868
  49.6 13.0 %copy-start.3 = (bf16[8,144,256]{2,1,0:T(8,128)(2,1)}, bf16[8,144,256]{2,1,0:T(8,128)(2,1)S(1)}, u32[]{:S(2)}) copy-start(bf16[8,144,256]{2,1,0:T(8,128)(2,1)S(1)} %collective-permute-done.13.refs_7_.rest_11_) | copy-start | bytes 1769476
  62.5 11.6 %copy-start.14 = (bf16[8,128,256]{2,1,0:T(8,128)(2,1)S(1)}, bf16[8,128,256]{2,1,0:T(8,128)(2,1)}, u32[]{:S(2)}) copy-start(bf16[8,128,256]{2,1,0:T(8,128)(2,1)} %copy-done.13) | copy-start | bytes 1572868
  63.3 61.6 %all-to-all-start = ((bf16[128,128,128]{2,1,0:T(8,128)(2,1)}), bf16[128,128,128]{2,1,0:T(8,128)(2,1)}, u32[]{:S(2)}, u32[]{:S(2)}) async-start(bf16[128,128,128]{2,1,0:T(8,128)(2,1)} %send_conf.1), calls=%async_computation | async-start | bytes 8388608 | tf_op jit(solution)/shard_map/all_to_all | solution.py:436
  73.5 7.5 %copy-start.4 = (bf16[8,144,256]{2,1,0:T(8,128)(2,1)S(1)}, bf16[8,144,256]{2,1,0:T(8,128)(2,1)}, u32[]{:S(2)}) copy-start(bf16[8,144,256]{2,1,0:T(8,128)(2,1)} %copy-done.3) | copy-start | bytes 1769476
  73.5 8.4 %copy-start.12 = (bf16[8,128,256]{2,1,0:T(8,128)(2,1)S(1)}, bf16[8,128,256]{2,1,0:T(8,128)(2,1)}, u32[]{:S(2)}) copy-start(bf16[8,128,256]{2,1,0:T(8,128)(2,1)} %copy-done.11) | copy-start | bytes 1572868
  73.6 8.6 %copy-start.10 = (bf16[8,128,256]{2,1,0:T(8,128)(2,1)S(1)}, bf16[8,128,256]{2,1,0:T(8,128)(2,1)}, u32[]{:S(2)}) copy-start(bf16[8,128,256]{2,1,0:T(8,128)(2,1)} %copy-done.9) | copy-start | bytes 1572868
  73.6 7.4 %collective-permute-start.19 = (bf16[8,144,256]{2,1,0:T(8,128)(2,1)S(1)}, bf16[8,144,256]{2,1,0:T(8,128)(2,1)S(1)}, u32[]{:S(2)}, u32[]{:S(2)}) collective-permute-start(bf16[8,144,256]{2,1,0:T(8,128)(2,1)S(1)} %constant_dynamic-update-slice_fusion.5.refs_4_.rest_8_), channel_id=1, source_target_pairs={{1,0},{0,1},{5,4},{4,5},{9,8},{8,9},{13,12},{12,13},{33,32},{32,33... | collective-permute-start | bytes 1769480 | tf_op jit(solution)/shard_map/ppermute | solution.py:49
  74.0 6.7 %collective-permute-start.15 = (bf16[8,128,256]{2,1,0:T(8,128)(2,1)S(1)}, bf16[8,128,256]{2,1,0:T(8,128)(2,1)S(1)}, u32[]{:S(2)}, u32[]{:S(2)}) collective-permute-start(bf16[8,128,256]{2,1,0:T(8,128)(2,1)S(1)} %constant_dynamic-update-slice_fusion.refs_0_.rest_0_), channel_id=1, source_target_pairs={{1,0},{0,1},{5,4},{4,5},{9,8},{8,9},{13,12},{12,13},{33,32},{32,33... | collective-permute-start | bytes 1572872 | tf_op jit(solution)/shard_map/ppermute | solution.py:49
  74.2 8.0 %collective-permute-start.16 = (bf16[8,128,256]{2,1,0:T(8,128)(2,1)S(1)}, bf16[8,128,256]{2,1,0:T(8,128)(2,1)S(1)}, u32[]{:S(2)}, u32[]{:S(2)}) collective-permute-start(bf16[8,128,256]{2,1,0:T(8,128)(2,1)S(1)} %copy-done.14), channel_id=1, source_target_pairs={{1,0},{0,1},{5,4},{4,5},{9,8},{8,9},{13,12},{12,13},{33,32},{32,33... | collective-permute-start | bytes 1572872 | tf_op jit(solution)/shard_map/ppermute | solution.py:49
  80.2 1.7 collective-permute-start.14
  80.4 5.4 %collective-permute-start.20 = (bf16[8,144,256]{2,1,0:T(8,128)(2,1)S(1)}, bf16[8,144,256]{2,1,0:T(8,128)(2,1)S(1)}, u32[]{:S(2)}, u32[]{:S(2)}) collective-permute-start(bf16[8,144,256]{2,1,0:T(8,128)(2,1)S(1)} %copy-done.8), channel_id=1, source_target_pairs={{1,0},{0,1},{5,4},{4,5},{9,8},{8,9},{13,12},{12,13},{33,32},{32,33... | collective-permute-start | bytes 1769480 | tf_op jit(solution)/shard_map/ppermute | solution.py:49
  80.7 5.1 %collective-permute-start.21 = (bf16[8,144,256]{2,1,0:T(8,128)(2,1)S(1)}, bf16[8,144,256]{2,1,0:T(8,128)(2,1)S(1)}, u32[]{:S(2)}, u32[]{:S(2)}) collective-permute-start(bf16[8,144,256]{2,1,0:T(8,128)(2,1)S(1)} %copy-done.6), channel_id=1, source_target_pairs={{1,0},{0,1},{5,4},{4,5},{9,8},{8,9},{13,12},{12,13},{33,32},{32,33... | collective-permute-start | bytes 1769480 | tf_op jit(solution)/shard_map/ppermute | solution.py:49
  81.0 4.8 %collective-permute-start.22 = (bf16[8,144,256]{2,1,0:T(8,128)(2,1)S(1)}, bf16[8,144,256]{2,1,0:T(8,128)(2,1)S(1)}, u32[]{:S(2)}, u32[]{:S(2)}) collective-permute-start(bf16[8,144,256]{2,1,0:T(8,128)(2,1)S(1)} %copy-done.4), channel_id=1, source_target_pairs={{1,0},{0,1},{5,4},{4,5},{9,8},{8,9},{13,12},{12,13},{33,32},{32,33... | collective-permute-start | bytes 1769480 | tf_op jit(solution)/shard_map/ppermute | solution.py:49
  81.9 3.1 %collective-permute-start.17 = (bf16[8,128,256]{2,1,0:T(8,128)(2,1)S(1)}, bf16[8,128,256]{2,1,0:T(8,128)(2,1)S(1)}, u32[]{:S(2)}, u32[]{:S(2)}) collective-permute-start(bf16[8,128,256]{2,1,0:T(8,128)(2,1)S(1)} %copy-done.12), channel_id=1, source_target_pairs={{1,0},{0,1},{5,4},{4,5},{9,8},{8,9},{13,12},{12,13},{33,32},{32,33... | collective-permute-start | bytes 1572872 | tf_op jit(solution)/shard_map/ppermute | solution.py:49
  82.2 3.6 %collective-permute-start.18 = (bf16[8,128,256]{2,1,0:T(8,128)(2,1)S(1)}, bf16[8,128,256]{2,1,0:T(8,128)(2,1)S(1)}, u32[]{:S(2)}, u32[]{:S(2)}) collective-permute-start(bf16[8,128,256]{2,1,0:T(8,128)(2,1)S(1)} %copy-done.10), channel_id=1, source_target_pairs={{1,0},{0,1},{5,4},{4,5},{9,8},{8,9},{13,12},{12,13},{33,32},{32,33... | collective-permute-start | bytes 1572872 | tf_op jit(solution)/shard_map/ppermute | solution.py:49
  124.9 8.5 %copy-start = (f32[256,256]{1,0:T(8,128)S(1)}, f32[256,256]{1,0:T(8,128)}, u32[]{:S(2)}) copy-start(f32[256,256]{1,0:T(8,128)} %get-tuple-element.27) | copy-start | bytes 786436
  124.9 112.0 %copy-start.24 = (bf16[512]{0:T(512)(128)(2,1)S(1)}, bf16[512]{0:T(512)(128)(2,1)}, u32[]{:S(2)}) copy-start(bf16[512]{0:T(512)(128)(2,1)} %param.7) | copy-start | bytes 3076
  124.9 116.4 %all-to-all-start.1 = ((bf16[128,128,256]{2,1,0:T(8,128)(2,1)}), bf16[128,128,256]{2,1,0:T(8,128)(2,1)}, u32[]{:S(2)}, u32[]{:S(2)}) async-start(bf16[128,128,256]{2,1,0:T(8,128)(2,1)} %get-tuple-element.26), calls=%async_computation.1 | async-start | bytes 16777216 | tf_op jit(solution)/shard_map/all_to_all | solution.py:436
  133.4 1.4 collective-permute-start.23
  134.9 95.8 %collective-permute-start.26 = (f32[128,256]{1,0:T(8,128)S(1)}, f32[128,256]{1,0:T(8,128)S(1)}, u32[]{:S(2)}, u32[]{:S(2)}) collective-permute-start(f32[128,256]{1,0:T(8,128)S(1)} %select_add_fusion), channel_id=1, source_target_pairs={{18,0},{19,1},{22,4},{23,5},{26,8},{27,9},{30,12},{31,13},{50,32},... | collective-permute-start | bytes 393224 | tf_op jit(solution)/shard_map/ppermute | solution.py:49
  135.2 95.4 %collective-permute-start.25 = (f32[128,256]{1,0:T(8,128)S(1)}, f32[128,256]{1,0:T(8,128)S(1)}, u32[]{:S(2)}, u32[]{:S(2)}) collective-permute-start(f32[128,256]{1,0:T(8,128)S(1)} %select_add_fusion), channel_id=1, source_target_pairs={{16,0},{17,1},{20,4},{21,5},{24,8},{25,9},{28,12},{29,13},{48,32},... | collective-permute-start | bytes 393224 | tf_op jit(solution)/shard_map/ppermute | solution.py:49
  136.4 96.4 %collective-permute-start.24 = (f32[128,256]{1,0:T(8,128)S(1)}, f32[128,256]{1,0:T(8,128)S(1)}, u32[]{:S(2)}, u32[]{:S(2)}) collective-permute-start(f32[128,256]{1,0:T(8,128)S(1)} %select_add_fusion), channel_id=1, source_target_pairs={{2,0},{3,1},{6,4},{7,5},{10,8},{11,9},{14,12},{15,13},{34,32},{35,... | collective-permute-start | bytes 393224 | tf_op jit(solution)/shard_map/ppermute | solution.py:49
  232.9 4.6 %collective-permute-start.29 = (f32[128,256]{1,0:T(8,128)S(1)}, f32[128,256]{1,0:T(8,128)S(1)}, u32[]{:S(2)}, u32[]{:S(2)}) collective-permute-start(f32[128,256]{1,0:T(8,128)S(1)} %add_add_fusion.2), channel_id=1, source_target_pairs={{96,0},{97,1},{100,4},{101,5},{104,8},{105,9},{108,12},{109,13},{0... | collective-permute-start | bytes 393224 | tf_op jit(solution)/shard_map/ppermute | solution.py:49
  233.0 5.4 %collective-permute-start.28 = (f32[128,256]{1,0:T(8,128)S(1)}, f32[128,256]{1,0:T(8,128)S(1)}, u32[]{:S(2)}, u32[]{:S(2)}) collective-permute-start(f32[128,256]{1,0:T(8,128)S(1)} %add_add_fusion.2), channel_id=1, source_target_pairs={{32,0},{33,1},{36,4},{37,5},{40,8},{41,9},{44,12},{45,13},{64,32},... | collective-permute-start | bytes 393224 | tf_op jit(solution)/shard_map/ppermute | solution.py:49
  234.4 6.9 %collective-permute-start.27 = (f32[128,256]{1,0:T(8,128)S(1)}, f32[128,256]{1,0:T(8,128)S(1)}, u32[]{:S(2)}, u32[]{:S(2)}) collective-permute-start(f32[128,256]{1,0:T(8,128)S(1)} %add_add_fusion.2), channel_id=1, source_target_pairs={{64,0},{65,1},{68,4},{69,5},{72,8},{73,9},{76,12},{77,13},{96,32},... | collective-permute-start | bytes 393224 | tf_op jit(solution)/shard_map/ppermute | solution.py:49
  252.4 9.5 %collective-permute-start.32 = (f32[128,256]{1,0:T(8,128)S(1)}, f32[128,256]{1,0:T(8,128)S(1)}, u32[]{:S(2)}, u32[]{:S(2)}) collective-permute-start(f32[128,256]{1,0:T(8,128)S(1)} %add_add_fusion.1), channel_id=1, source_target_pairs={{12,0},{13,1},{0,4},{1,5},{4,8},{5,9},{8,12},{9,13},{44,32},{45,33... | collective-permute-start | bytes 393224 | tf_op jit(solution)/shard_map/ppermute | solution.py:49
  259.1 3.8 %collective-permute-start.31 = (f32[128,256]{1,0:T(8,128)S(1)}, f32[128,256]{1,0:T(8,128)S(1)}, u32[]{:S(2)}, u32[]{:S(2)}) collective-permute-start(f32[128,256]{1,0:T(8,128)S(1)} %add_add_fusion.1), channel_id=1, source_target_pairs={{4,0},{5,1},{8,4},{9,5},{12,8},{13,9},{0,12},{1,13},{36,32},{37,33... | collective-permute-start | bytes 393224 | tf_op jit(solution)/shard_map/ppermute | solution.py:49
  259.2 6.4 %collective-permute-start.30 = (f32[128,256]{1,0:T(8,128)S(1)}, f32[128,256]{1,0:T(8,128)S(1)}, u32[]{:S(2)}, u32[]{:S(2)}) collective-permute-start(f32[128,256]{1,0:T(8,128)S(1)} %add_add_fusion.1), channel_id=1, source_target_pairs={{8,0},{9,1},{12,4},{13,5},{0,8},{1,9},{4,12},{5,13},{40,32},{41,33... | collective-permute-start | bytes 393224 | tf_op jit(solution)/shard_map/ppermute | solution.py:49
  265.6 3.7 %collective-permute-start.33 = (f32[128,256]{1,0:T(8,128)S(1)}, f32[128,256]{1,0:T(8,128)S(1)}, u32[]{:S(2)}, u32[]{:S(2)}) collective-permute-start(f32[128,256]{1,0:T(8,128)S(1)} %add_add_fusion), channel_id=1, source_target_pairs={{1,0},{0,1},{5,4},{4,5},{9,8},{8,9},{13,12},{12,13},{33,32},{32,33... | collective-permute-start | bytes 393224 | tf_op jit(solution)/shard_map/ppermute | solution.py:49
  (13 other events, 39.3 us)

commit v3 on v2

--- a/solution.py
+++ b/solution.py
@@ -343,7 +343,7 @@
             target[...] += nn(weights, part)
             return carry
 
-        lax.fori_loop(0, CHUNKS, step, 0, unroll=2)
+        lax.fori_loop(0, CHUNKS, step, 0, unroll=4)
 
     def add_returned(target, narrow, waits=False):
         level_wide = jnp.concatenate([level] * ITEM_GROUP, axis=1)
@@ -356,7 +356,7 @@
             target[...] += nn((excess * scores).astype(BF), part)
             return carry
 
-        lax.fori_loop(0, CHUNKS, step, 0, unroll=2)
+        lax.fori_loop(0, CHUNKS, step, 0, unroll=4)
 
     return level, add_right, add_returned
 
@@ -441,7 +441,7 @@
     first = values[:rows]
     second = values[rows:]
     half = jnp.where(core == 0, first, second) + fetch(jnp.where(core == 0, second, first), flip=1)
-    return sum_axis(sum_axis(half, "dx"), "dy")
+    return sum_axis(half, "dx")
 
 
 def sum_axis(half, axis):
@@ -473,6 +473,7 @@
     line_a = jnp.concatenate([part_a] + [fetch(part_a, dy=d) for d in OFFSETS[1:]], axis=0)
     line_b = jnp.concatenate([part_b] + [fetch(part_b, dz=d) for d in OFFSETS[1:]], axis=0)
     send_conf = send_conf_of(items, tile_count, conf_tiles)
+    line_a, line_b = lax.optimization_barrier((line_a, line_b))
     full_a = [line_a] + [fetch(line_a, dz=d) for d in OFFSETS[1:]]
     full_b = [line_b] + [fetch(line_b, dy=d) for d in OFFSETS[1:]]
     full_a[1:], full_b[1:], send_conf = lax.optimization_barrier(
@@ -491,7 +492,9 @@
     half_gram = sum_lines(local_gram, core)
     own = lax.dynamic_slice_in_dim(exposure, lax.axis_index("grp") * BS, BS)
     own = own.astype(F32).reshape(1, BS)
+    half_gram, got_rows, got_conf = lax.optimization_barrier((half_gram, got_rows, got_conf))
     right, returned = item_start(got_conf, got_rows, own)
+    half_gram = sum_axis(half_gram, "dy")
     half_gram, right, returned = lax.optimization_barrier((half_gram, right, returned))
     user_gram = sum_rest(half_gram, core) * (1.0 / (UB * BS))
     item_update = item_half(got_conf, got_rows, own, user_gram, right, returned)

time: 288 us -> 273 us (0.948)
  waiting for transfers between devices: 153 us -> 143 us
    ppermute x34, waiting for transfers between devices: 138 us -> 123 us  [fetch(): return lax.ppermute(values, BOTH, from_offset(**offset))]
    all_to_all x2, waiting for transfers between devices: 15 us -> 20.4 us  [exchange(): return lax.all_to_all(values, axes, split_axis=0, concat_axis=0, tiled=True)]
  transfers between devices with their start and end apart: 36 -> 36, of which waited for: 17 -> 17; matrix products, arithmetic and copies ran while one was open for 1% -> 1% of each run, Pallas kernels for 13% -> 17%
where the time goes in v3:
time: 273 us; the launch traced here: 271 us
  waiting for transfers between devices  143 us (52%)
  starting transfers between devices  60.8 us (22%)
  Pallas kernels  59.3 us (22%)
  local copies, waits for them, and re-layouts  4.77 us (2%)
    ppermute x34, waiting for transfers between devices, fetch(): return lax.ppermute(values, BOTH, from_offset(**offset))  123 us
    ppermute x34, starting transfers between devices, fetch(): return lax.ppermute(values, BOTH, from_offset(**offset))  43.2 us
    pallas_call x2, Pallas kernels, item_call(): pl.pallas_call(kernel, out_shape=outs, in_specs=[far, far] + [vmem] * len...  23.4 us
    pallas_call x1, Pallas kernels, user_half(): pl.pallas_call(user_kernel, out_shape=(jax.ShapeDtypeStruct((UB * BS, RAN...  22.8 us
    all_to_all x2, waiting for transfers between devices, exchange(): return lax.all_to_all(values, axes, split_axis=0, concat_axis=0, tiled=True)  20.4 us
    all_to_all x2, starting transfers between devices, exchange(): return lax.all_to_all(values, axes, split_axis=0, concat_axis=0, tiled=True)  17.5 us
    pallas_call x1, Pallas kernels, send_conf_of(): pl.pallas_call(send_kernel, out_shape=jax.ShapeDtypeStruct((TILES, BS, BS...  7.4 us
    pallas_call x1, Pallas kernels, gram_half(): pl.pallas_call(gram_kernel, out_shape=jax.ShapeDtypeStruct((RANK, RANK),...  5.65 us
  transfers between devices with their start and end apart: 36, of which 17 were waited for; matrix products, arithmetic and copies ran while one was open for 1% of the time, Pallas kernels for 17%

profile of v3, /device:TPU:15, one launch (start us, length us, event | category | flops | bytes accessed | tf_op | source)
XLA Modules:
  0.0 271.4 jit_solution(17863558589060720800)
XLA Ops:
  0.6 0.8 dynamic_slice.10
  1.4 0.8 constant_dynamic-slice_fusion
  2.2 0.6 collective-permute-start
  2.9 0.9 constant_dynamic-update-slice_fusion.9
  3.8 2.2 collective-permute-start.4
  6.0 0.7 collective-permute-done
  6.7 2.1 collective-permute-start.3
  8.8 1.5 collective-permute-start.1
  10.3 3.7 %collective-permute-start.7 = (bf16[2,144,256]{2,1,0:T(8,128)(2,1)S(1)}, bf16[2,144,256]{2,1,0:T(8,128)(2,1)S(1)}, u32[]{:S(2)}, u32[]{:S(2)}) collective-permute-start(bf16[2,144,256]{2,1,0:T(8,128)(2,1)S(1)} %pad_maximum_fusion), channel_id=1, source_target_pairs={{8,0},{9,1},{12,4},{13,5},{0,8},{1,9},{4,12},{5,13},{40,32},{41,33... | collective-permute-start | bytes 442376 | tf_op jit(solution)/shard_map/ppermute | solution.py:49
  13.9 0.7 collective-permute-start.6
  14.7 3.6 %collective-permute-start.5 = (bf16[2,144,256]{2,1,0:T(8,128)(2,1)S(1)}, bf16[2,144,256]{2,1,0:T(8,128)(2,1)S(1)}, u32[]{:S(2)}, u32[]{:S(2)}) collective-permute-start(bf16[2,144,256]{2,1,0:T(8,128)(2,1)S(1)} %pad_maximum_fusion), channel_id=1, source_target_pairs={{4,0},{5,1},{8,4},{9,5},{12,8},{13,9},{0,12},{1,13},{36,32},{37,33... | collective-permute-start | bytes 442376 | tf_op jit(solution)/shard_map/ppermute | solution.py:49
  18.4 2.8 %collective-permute-done.5 = bf16[2,144,256]{2,1,0:T(8,128)(2,1)S(1)} collective-permute-done((bf16[2,144,256]{2,1,0:T(8,128)(2,1)S(1)}, bf16[2,144,256]{2,1,0:T(8,128)(2,1)S(1)}, u32[]{:S(2)}, u32[]{:S(2)}) %collective-permute-start.5) | collective-permute-done | bytes 147488 | tf_op jit(solution)/shard_map/ppermute | solution.py:49
  21.3 2.0 collective-permute-start.10
  23.3 2.4 collective-permute-start.13
  26.2 0.9 collective-permute-start.11
  27.1 1.9 collective-permute-start.9
  29.1 4.8 %collective-permute-done.10.refs_3_.rest_3_ = bf16[8,128,256]{2,1,0:T(8,128)(2,1)S(1)} collective-permute-done((bf16[8,128,256]{2,1,0:T(8,128)(2,1)S(1)}, bf16[8,128,256]{2,1,0:T(8,128)(2,1)S(1)}, u32[]{:S(2)}, u32[]{:S(2)}) %collective-permute-start.10) | collective-permute-done | bytes 524320 | tf_op jit(solution)/shard_map/ppermute | solution.py:49
  33.9 2.8 %collective-permute-start.8 = (bf16[8,128,256]{2,1,0:T(8,128)(2,1)S(1)}, bf16[8,128,256]{2,1,0:T(8,128)(2,1)S(1)}, u32[]{:S(2)}, u32[]{:S(2)}) collective-permute-start(bf16[8,128,256]{2,1,0:T(8,128)(2,1)S(1)} %constant_dynamic-update-slice_fusion.refs_0_.rest_0_), channel_id=1, source_target_pairs={{4,0},{5,1},{8,4},{9,5},{12,8},{13,9},{0,12},{1,13},{36,32},{37,33... | collective-permute-start | bytes 1572872 | tf_op jit(solution)/shard_map/ppermute | solution.py:49
  37.3 7.4 %send_conf.1 = bf16[128,128,128]{2,1,0:T(8,128)(2,1)} custom-call(s32[128]{0:T(128)} %bitcast.20, s32[1]{0:T(128)S(6)} %copy.17.count, bf16[128,128,128]{2,1,0:T(8,128)(2,1)} %bitcast.15), custom_call_target="tpu_custom_call" | custom-call | bytes 16000000 | tf_op jit(solution)/shard_map/send_conf/pallas_call | solution.py:81
  44.7 2.1 collective-permute-done.9.refs_2_.rest_2_
  46.9 4.0 %collective-permute-done.12.refs_6_.rest_10_ = bf16[8,144,256]{2,1,0:T(8,128)(2,1)S(1)} collective-permute-done((bf16[8,144,256]{2,1,0:T(8,128)(2,1)S(1)}, bf16[8,144,256]{2,1,0:T(8,128)(2,1)S(1)}, u32[]{:S(2)}, u32[]{:S(2)}) %collective-permute-start.12) | collective-permute-done | bytes 589856 | tf_op jit(solution)/shard_map/ppermute | solution.py:49
  50.9 1.7 collective-permute-done.11.refs_5_.rest_9_
  52.7 0.8 copy-done.7
  53.5 9.1 %all-to-all-start.1 = ((bf16[128,128,128]{2,1,0:T(8,128)(2,1)}), bf16[128,128,128]{2,1,0:T(8,128)(2,1)}, u32[]{:S(2)}, u32[]{:S(2)}) async-start(bf16[128,128,128]{2,1,0:T(8,128)(2,1)} %send_conf.1), calls=%async_computation.1 | async-start | bytes 8388608 | tf_op jit(solution)/shard_map/all_to_all | solution.py:436
  63.6 5.7 %gram_half.1.gram_here = f32[256,256]{1,0:T(8,128)} custom-call(bf16[8,128,256]{2,1,0:T(8,128)(2,1)} %copy-done.2, bf16[8,128,256]{2,1,0:T(8,128)(2,1)} %copy-done.13, bf16[8,128,256]{2,1,0:T(8,128)(2,1)} %copy-done.11, bf16[8,128,256]{2,1,0:T(8,128)(2,1)} %copy-done.9, bf16[8,144,256]{2,1,0:T(8,128)(2,1)} %copy-done.1, bf16[8,144,256]{2,1,0:T(8,128)(2,1)} %copy-done.7, ...), custom_call_target="tpu_custom_call" | custom-call | flops 1000000000 | bytes 1000000 | tf_op jit(solution)/shard_map/gram_half/pallas_call | solution.py:268
  71.6 2.5 collective-permute-done.17.rest_6_
  74.0 0.7 collective-permute-done.18.rest_7_
  74.9 0.7 copy-done.22
  76.2 22.8 %user_half.1 = (bf16[512,256]{1,0:T(8,128)(2,1)}, bf16[128,128,256]{2,1,0:T(8,128)(2,1)}, f32[256,256]{1,0:T(8,128)}) custom-call(s32[128]{0:T(128)} %bitcast.21, s32[128]{0:T(128)} %bitcast.22, s32[1]{0:T(128)S(6)} %copy.17.count, f32[256,256]{1,0:T(8,128)} %gram_half.1.gram_here, f32[256,256]{1,0:T(8,128)} %copy-done.23, bf16[128,128,128]{2,1,0:T(8,128)(2,1)} %bitcast.16, ...), custom_call_target="tpu_custom_call" | custom-call | flops 5000000000 | bytes 4000000 | tf_op jit(solution)/shard_map/user_half/pallas_call | solution.py:284
  99.0 14.9 %all-to-all-done.1.conf_hbm = bf16[128,128,128]{2,1,0:T(8,128)(2,1)} async-done(((bf16[128,128,128]{2,1,0:T(8,128)(2,1)}), bf16[128,128,128]{2,1,0:T(8,128)(2,1)}, u32[]{:S(2)}, u32[]{:S(2)}) %all-to-all-start.1) | async-done | bytes 4194336 | tf_op jit(solution)/shard_map/all_to_all | solution.py:436
  113.9 8.5 %all-to-all-start = ((bf16[128,128,256]{2,1,0:T(8,128)(2,1)}), bf16[128,128,256]{2,1,0:T(8,128)(2,1)}, u32[]{:S(2)}, u32[]{:S(2)}) async-start(bf16[128,128,256]{2,1,0:T(8,128)(2,1)} %get-tuple-element.33), calls=%async_computation | async-start | bytes 16777216 | tf_op jit(solution)/shard_map/all_to_all | solution.py:436
  122.9 1.0 collective-permute-done.23
  124.3 1.2 collective-permute-start.25
  125.5 1.2 collective-permute-start.24
  127.2 92.5 %collective-permute-done.26 = f32[128,256]{1,0:T(8,128)S(1)} collective-permute-done((f32[128,256]{1,0:T(8,128)S(1)}, f32[128,256]{1,0:T(8,128)S(1)}, u32[]{:S(2)}, u32[]{:S(2)}) %collective-permute-start.26) | collective-permute-done | bytes 131104 | tf_op jit(solution)/shard_map/ppermute | solution.py:49
  219.7 2.2 collective-permute-done.24
  221.9 5.4 %all-to-all-done.rows_hbm = bf16[128,128,256]{2,1,0:T(8,128)(2,1)} async-done(((bf16[128,128,256]{2,1,0:T(8,128)(2,1)}), bf16[128,128,256]{2,1,0:T(8,128)(2,1)}, u32[]{:S(2)}, u32[]{:S(2)}) %all-to-all-start) | async-done | bytes 8388640 | tf_op jit(solution)/shard_map/all_to_all | solution.py:436
  227.3 4.0 %collective-permute-start.28 = (f32[128,256]{1,0:T(8,128)S(1)}, f32[128,256]{1,0:T(8,128)S(1)}, u32[]{:S(2)}, u32[]{:S(2)}) collective-permute-start(f32[128,256]{1,0:T(8,128)S(1)} %add_add_fusion.2), channel_id=1, source_target_pairs={{32,0},{33,1},{36,4},{37,5},{40,8},{41,9},{44,12},{45,13},{64,32},... | collective-permute-start | bytes 393224 | tf_op jit(solution)/shard_map/ppermute | solution.py:49
  231.4 1.8 collective-permute-start.27
  233.1 10.5 %item_start.1 = (f32[128,256]{1,0:T(8,128)}, f32[128,256]{1,0:T(8,128)}) custom-call(bf16[128,128,128]{2,1,0:T(8,128)(2,1)} %all-to-all-done.1.conf_hbm, bf16[128,128,256]{2,1,0:T(8,128)(2,1)} %all-to-all-done.rows_hbm, f32[1,128]{1,0:T(1,128)} %bitcast_convert_fusion.exposure), custom_call_target="tpu_custom_call" | custom-call | flops 12000000000 | bytes 13000000 | tf_op jit(solution)/shard_map/item_start/pallas_call | solution.py:404
  243.8 4.0 %collective-permute-start.31 = (f32[128,256]{1,0:T(8,128)S(1)}, f32[128,256]{1,0:T(8,128)S(1)}, u32[]{:S(2)}, u32[]{:S(2)}) collective-permute-start(f32[128,256]{1,0:T(8,128)S(1)} %add_add_fusion.1), channel_id=1, source_target_pairs={{4,0},{5,1},{8,4},{9,5},{12,8},{13,9},{0,12},{1,13},{36,32},{37,33... | collective-permute-start | bytes 393224 | tf_op jit(solution)/shard_map/ppermute | solution.py:49
  247.9 1.1 collective-permute-start.30
  249.0 1.8 collective-permute-done.32
  250.8 4.4 %collective-permute-done.30 = f32[128,256]{1,0:T(8,128)S(1)} collective-permute-done((f32[128,256]{1,0:T(8,128)S(1)}, f32[128,256]{1,0:T(8,128)S(1)}, u32[]{:S(2)}, u32[]{:S(2)}) %collective-permute-start.30) | collective-permute-done | bytes 131104 | tf_op jit(solution)/shard_map/ppermute | solution.py:49
  255.2 1.4 collective-permute-start.33
  256.6 1.0 collective-permute-done.33
  257.6 0.7 maximum_multiply_fusion.user_gram
  258.3 12.9 %item_half.1 = bf16[128,256]{1,0:T(8,128)(2,1)} custom-call(bf16[128,128,128]{2,1,0:T(8,128)(2,1)} %all-to-all-done.1.conf_hbm, bf16[128,128,256]{2,1,0:T(8,128)(2,1)} %all-to-all-done.rows_hbm, f32[1,128]{1,0:T(1,128)} %bitcast_convert_fusion.exposure, f32[256,256]{1,0:T(8,128)} %maximum_multiply_fusion.user_gram, f32[128,256]{1,0:T(8,128)} %get-tuple-element.41.right, ...), custom_call_target="tpu_custom_call" | custom-call | flops 12000000000 | bytes 13000000 | tf_op jit(solution)/shard_map/item_half/pallas_call | solution.py:404
  (103 shorter events, 6.4 us)
Async XLA Ops:
  2.2 4.4 %collective-permute-start = (bf16[128,256]{1,0:T(8,128)(2,1)S(1)}, bf16[128,256]{1,0:T(8,128)(2,1)S(1)}, u32[]{:S(2)}, u32[]{:S(2)}) collective-permute-start(bf16[128,256]{1,0:T(8,128)(2,1)S(1)} %get-tuple-element.48), channel_id=1, source_target_pairs={{16,0},{17,1},{20,4},{21,5},{24,8},{25,9},{28,12},{29,13},{48,32},... | collective-permute-start | bytes 196616 | tf_op jit(solution)/shard_map/ppermute | solution.py:49
  3.8 6.5 %collective-permute-start.4 = (bf16[144,256]{1,0:T(8,128)(2,1)S(1)}, bf16[144,256]{1,0:T(8,128)(2,1)S(1)}, u32[]{:S(2)}, u32[]{:S(2)}) collective-permute-start(bf16[144,256]{1,0:T(8,128)(2,1)S(1)} %get-tuple-element.44), channel_id=1, source_target_pairs={{18,0},{19,1},{22,4},{23,5},{26,8},{27,9},{30,12},{31,13},{50,32},... | collective-permute-start | bytes 221192 | tf_op jit(solution)/shard_map/ppermute | solution.py:49
  6.7 11.7 %collective-permute-start.3 = (bf16[2,128,256]{2,1,0:T(8,128)(2,1)S(1)}, bf16[2,128,256]{2,1,0:T(8,128)(2,1)S(1)}, u32[]{:S(2)}, u32[]{:S(2)}) collective-permute-start(bf16[2,128,256]{2,1,0:T(8,128)(2,1)S(1)} %pad_maximum_fusion.1), channel_id=1, source_target_pairs={{64,0},{65,1},{68,4},{69,5},{72,8},{73,9},{76,12},{77,13},{96,32},... | collective-permute-start | bytes 393224 | tf_op jit(solution)/shard_map/ppermute | solution.py:49
  8.7 9.6 %collective-permute-start.2 = (bf16[2,128,256]{2,1,0:T(8,128)(2,1)S(1)}, bf16[2,128,256]{2,1,0:T(8,128)(2,1)S(1)}, u32[]{:S(2)}, u32[]{:S(2)}) collective-permute-start(bf16[2,128,256]{2,1,0:T(8,128)(2,1)S(1)} %pad_maximum_fusion.1), channel_id=1, source_target_pairs={{96,0},{97,1},{100,4},{101,5},{104,8},{105,9},{108,12},{109,13},{0... | collective-permute-start | bytes 393224 | tf_op jit(solution)/shard_map/ppermute | solution.py:49
  8.8 5.9 %collective-permute-start.1 = (bf16[2,128,256]{2,1,0:T(8,128)(2,1)S(1)}, bf16[2,128,256]{2,1,0:T(8,128)(2,1)S(1)}, u32[]{:S(2)}, u32[]{:S(2)}) collective-permute-start(bf16[2,128,256]{2,1,0:T(8,128)(2,1)S(1)} %pad_maximum_fusion.1), channel_id=1, source_target_pairs={{32,0},{33,1},{36,4},{37,5},{40,8},{41,9},{44,12},{45,13},{64,32},... | collective-permute-start | bytes 393224 | tf_op jit(solution)/shard_map/ppermute | solution.py:49
  10.3 11.0 %collective-permute-start.7 = (bf16[2,144,256]{2,1,0:T(8,128)(2,1)S(1)}, bf16[2,144,256]{2,1,0:T(8,128)(2,1)S(1)}, u32[]{:S(2)}, u32[]{:S(2)}) collective-permute-start(bf16[2,144,256]{2,1,0:T(8,128)(2,1)S(1)} %pad_maximum_fusion), channel_id=1, source_target_pairs={{8,0},{9,1},{12,4},{13,5},{0,8},{1,9},{4,12},{5,13},{40,32},{41,33... | collective-permute-start | bytes 442376 | tf_op jit(solution)/shard_map/ppermute | solution.py:49
  13.9 7.3 %collective-permute-start.6 = (bf16[2,144,256]{2,1,0:T(8,128)(2,1)S(1)}, bf16[2,144,256]{2,1,0:T(8,128)(2,1)S(1)}, u32[]{:S(2)}, u32[]{:S(2)}) collective-permute-start(bf16[2,144,256]{2,1,0:T(8,128)(2,1)S(1)} %pad_maximum_fusion), channel_id=1, source_target_pairs={{12,0},{13,1},{0,4},{1,5},{4,8},{5,9},{8,12},{9,13},{44,32},{45,33... | collective-permute-start | bytes 442376 | tf_op jit(solution)/shard_map/ppermute | solution.py:49
  14.7 6.5 %collective-permute-start.5 = (bf16[2,144,256]{2,1,0:T(8,128)(2,1)S(1)}, bf16[2,144,256]{2,1,0:T(8,128)(2,1)S(1)}, u32[]{:S(2)}, u32[]{:S(2)}) collective-permute-start(bf16[2,144,256]{2,1,0:T(8,128)(2,1)S(1)} %pad_maximum_fusion), channel_id=1, source_target_pairs={{4,0},{5,1},{8,4},{9,5},{12,8},{13,9},{0,12},{1,13},{36,32},{37,33... | collective-permute-start | bytes 442376 | tf_op jit(solution)/shard_map/ppermute | solution.py:49
  18.4 44.7 %copy-start.2 = (bf16[8,128,256]{2,1,0:T(8,128)(2,1)}, bf16[8,128,256]{2,1,0:T(8,128)(2,1)S(1)}, u32[]{:S(2)}) copy-start(bf16[8,128,256]{2,1,0:T(8,128)(2,1)S(1)} %constant_dynamic-update-slice_fusion.refs_0_.rest_0_) | copy-start | bytes 1572868
  21.3 41.3 %copy-start.1 = (bf16[8,144,256]{2,1,0:T(8,128)(2,1)}, bf16[8,144,256]{2,1,0:T(8,128)(2,1)S(1)}, u32[]{:S(2)}) copy-start(bf16[8,144,256]{2,1,0:T(8,128)(2,1)S(1)} %constant_dynamic-update-slice_fusion.5.refs_4_.rest_8_) | copy-start | bytes 1769476
  21.3 12.6 %collective-permute-start.10 = (bf16[8,128,256]{2,1,0:T(8,128)(2,1)S(1)}, bf16[8,128,256]{2,1,0:T(8,128)(2,1)S(1)}, u32[]{:S(2)}, u32[]{:S(2)}) collective-permute-start(bf16[8,128,256]{2,1,0:T(8,128)(2,1)S(1)} %constant_dynamic-update-slice_fusion.refs_0_.rest_0_), channel_id=1, source_target_pairs={{8,0},{9,1},{12,4},{13,5},{0,8},{1,9},{4,12},{5,13},{40,32},{41,33... | collective-permute-start | bytes 1572872 | tf_op jit(solution)/shard_map/ppermute | solution.py:49
  23.3 23.6 %collective-permute-start.13 = (bf16[8,144,256]{2,1,0:T(8,128)(2,1)S(1)}, bf16[8,144,256]{2,1,0:T(8,128)(2,1)S(1)}, u32[]{:S(2)}, u32[]{:S(2)}) collective-permute-start(bf16[8,144,256]{2,1,0:T(8,128)(2,1)S(1)} %constant_dynamic-update-slice_fusion.5.refs_4_.rest_8_), channel_id=1, source_target_pairs={{64,0},{65,1},{68,4},{69,5},{72,8},{73,9},{76,12},{77,13},{96,32},... | collective-permute-start | bytes 1769480 | tf_op jit(solution)/shard_map/ppermute | solution.py:49
  25.6 25.2 %collective-permute-start.12 = (bf16[8,144,256]{2,1,0:T(8,128)(2,1)S(1)}, bf16[8,144,256]{2,1,0:T(8,128)(2,1)S(1)}, u32[]{:S(2)}, u32[]{:S(2)}) collective-permute-start(bf16[8,144,256]{2,1,0:T(8,128)(2,1)S(1)} %constant_dynamic-update-slice_fusion.5.refs_4_.rest_8_), channel_id=1, source_target_pairs={{96,0},{97,1},{100,4},{101,5},{104,8},{105,9},{108,12},{109,13},{0... | collective-permute-start | bytes 1769480 | tf_op jit(solution)/shard_map/ppermute | solution.py:49
  26.2 26.4 %collective-permute-start.11 = (bf16[8,144,256]{2,1,0:T(8,128)(2,1)S(1)}, bf16[8,144,256]{2,1,0:T(8,128)(2,1)S(1)}, u32[]{:S(2)}, u32[]{:S(2)}) collective-permute-start(bf16[8,144,256]{2,1,0:T(8,128)(2,1)S(1)} %constant_dynamic-update-slice_fusion.5.refs_4_.rest_8_), channel_id=1, source_target_pairs={{32,0},{33,1},{36,4},{37,5},{40,8},{41,9},{44,12},{45,13},{64,32},... | collective-permute-start | bytes 1769480 | tf_op jit(solution)/shard_map/ppermute | solution.py:49
  27.1 19.8 %collective-permute-start.9 = (bf16[8,128,256]{2,1,0:T(8,128)(2,1)S(1)}, bf16[8,128,256]{2,1,0:T(8,128)(2,1)S(1)}, u32[]{:S(2)}, u32[]{:S(2)}) collective-permute-start(bf16[8,128,256]{2,1,0:T(8,128)(2,1)S(1)} %constant_dynamic-update-slice_fusion.refs_0_.rest_0_), channel_id=1, source_target_pairs={{12,0},{13,1},{0,4},{1,5},{4,8},{5,9},{8,12},{9,13},{44,32},{45,33... | collective-permute-start | bytes 1572872 | tf_op jit(solution)/shard_map/ppermute | solution.py:49
  33.9 10.9 %copy-start.9 = (bf16[8,128,256]{2,1,0:T(8,128)(2,1)}, bf16[8,128,256]{2,1,0:T(8,128)(2,1)S(1)}, u32[]{:S(2)}) copy-start(bf16[8,128,256]{2,1,0:T(8,128)(2,1)S(1)} %collective-permute-done.10.refs_3_.rest_3_) | copy-start | bytes 1572868
  33.9 13.0 %collective-permute-start.8 = (bf16[8,128,256]{2,1,0:T(8,128)(2,1)S(1)}, bf16[8,128,256]{2,1,0:T(8,128)(2,1)S(1)}, u32[]{:S(2)}, u32[]{:S(2)}) collective-permute-start(bf16[8,128,256]{2,1,0:T(8,128)(2,1)S(1)} %constant_dynamic-update-slice_fusion.refs_0_.rest_0_), channel_id=1, source_target_pairs={{4,0},{5,1},{8,4},{9,5},{12,8},{13,9},{0,12},{1,13},{36,32},{37,33... | collective-permute-start | bytes 1572872 | tf_op jit(solution)/shard_map/ppermute | solution.py:49
  46.9 5.8 %copy-start.3 = (bf16[8,144,256]{2,1,0:T(8,128)(2,1)}, bf16[8,144,256]{2,1,0:T(8,128)(2,1)S(1)}, u32[]{:S(2)}) copy-start(bf16[8,144,256]{2,1,0:T(8,128)(2,1)S(1)} %collective-permute-done.13.refs_7_.rest_11_) | copy-start | bytes 1769476
  52.7 10.5 %copy-start.14 = (bf16[8,128,256]{2,1,0:T(8,128)(2,1)S(1)}, bf16[8,128,256]{2,1,0:T(8,128)(2,1)}, u32[]{:S(2)}) copy-start(bf16[8,128,256]{2,1,0:T(8,128)(2,1)} %copy-done.13) | copy-start | bytes 1572868
  53.5 60.5 %all-to-all-start.1 = ((bf16[128,128,128]{2,1,0:T(8,128)(2,1)}), bf16[128,128,128]{2,1,0:T(8,128)(2,1)}, u32[]{:S(2)}, u32[]{:S(2)}) async-start(bf16[128,128,128]{2,1,0:T(8,128)(2,1)} %send_conf.1), calls=%async_computation.1 | async-start | bytes 8388608 | tf_op jit(solution)/shard_map/all_to_all | solution.py:436
  62.6 6.9 %copy-start.8 = (bf16[8,144,256]{2,1,0:T(8,128)(2,1)S(1)}, bf16[8,144,256]{2,1,0:T(8,128)(2,1)}, u32[]{:S(2)}) copy-start(bf16[8,144,256]{2,1,0:T(8,128)(2,1)} %copy-done.7) | copy-start | bytes 1769476
  62.6 7.2 %copy-start.6 = (bf16[8,144,256]{2,1,0:T(8,128)(2,1)S(1)}, bf16[8,144,256]{2,1,0:T(8,128)(2,1)}, u32[]{:S(2)}) copy-start(bf16[8,144,256]{2,1,0:T(8,128)(2,1)} %copy-done.5) | copy-start | bytes 1769476
  62.6 7.5 %copy-start.4 = (bf16[8,144,256]{2,1,0:T(8,128)(2,1)S(1)}, bf16[8,144,256]{2,1,0:T(8,128)(2,1)}, u32[]{:S(2)}) copy-start(bf16[8,144,256]{2,1,0:T(8,128)(2,1)} %copy-done.3) | copy-start | bytes 1769476
  62.6 8.4 %copy-start.12 = (bf16[8,128,256]{2,1,0:T(8,128)(2,1)S(1)}, bf16[8,128,256]{2,1,0:T(8,128)(2,1)}, u32[]{:S(2)}) copy-start(bf16[8,128,256]{2,1,0:T(8,128)(2,1)} %copy-done.11) | copy-start | bytes 1572868
  62.6 8.6 %copy-start.10 = (bf16[8,128,256]{2,1,0:T(8,128)(2,1)S(1)}, bf16[8,128,256]{2,1,0:T(8,128)(2,1)}, u32[]{:S(2)}) copy-start(bf16[8,128,256]{2,1,0:T(8,128)(2,1)} %copy-done.9) | copy-start | bytes 1572868
  62.6 7.4 %collective-permute-start.19 = (bf16[8,144,256]{2,1,0:T(8,128)(2,1)S(1)}, bf16[8,144,256]{2,1,0:T(8,128)(2,1)S(1)}, u32[]{:S(2)}, u32[]{:S(2)}) collective-permute-start(bf16[8,144,256]{2,1,0:T(8,128)(2,1)S(1)} %constant_dynamic-update-slice_fusion.5.refs_4_.rest_8_), channel_id=1, source_target_pairs={{1,0},{0,1},{5,4},{4,5},{9,8},{8,9},{13,12},{12,13},{33,32},{32,33... | collective-permute-start | bytes 1769480 | tf_op jit(solution)/shard_map/ppermute | solution.py:49
  63.0 6.7 %collective-permute-start.15 = (bf16[8,128,256]{2,1,0:T(8,128)(2,1)S(1)}, bf16[8,128,256]{2,1,0:T(8,128)(2,1)S(1)}, u32[]{:S(2)}, u32[]{:S(2)}) collective-permute-start(bf16[8,128,256]{2,1,0:T(8,128)(2,1)S(1)} %constant_dynamic-update-slice_fusion.refs_0_.rest_0_), channel_id=1, source_target_pairs={{1,0},{0,1},{5,4},{4,5},{9,8},{8,9},{13,12},{12,13},{33,32},{32,33... | collective-permute-start | bytes 1572872 | tf_op jit(solution)/shard_map/ppermute | solution.py:49
  63.2 8.0 %collective-permute-start.16 = (bf16[8,128,256]{2,1,0:T(8,128)(2,1)S(1)}, bf16[8,128,256]{2,1,0:T(8,128)(2,1)S(1)}, u32[]{:S(2)}, u32[]{:S(2)}) collective-permute-start(bf16[8,128,256]{2,1,0:T(8,128)(2,1)S(1)} %copy-done.14), channel_id=1, source_target_pairs={{1,0},{0,1},{5,4},{4,5},{9,8},{8,9},{13,12},{12,13},{33,32},{32,33... | collective-permute-start | bytes 1572872 | tf_op jit(solution)/shard_map/ppermute | solution.py:49
  69.2 1.7 collective-permute-start.14
  69.4 5.4 %collective-permute-start.20 = (bf16[8,144,256]{2,1,0:T(8,128)(2,1)S(1)}, bf16[8,144,256]{2,1,0:T(8,128)(2,1)S(1)}, u32[]{:S(2)}, u32[]{:S(2)}) collective-permute-start(bf16[8,144,256]{2,1,0:T(8,128)(2,1)S(1)} %copy-done.8), channel_id=1, source_target_pairs={{1,0},{0,1},{5,4},{4,5},{9,8},{8,9},{13,12},{12,13},{33,32},{32,33... | collective-permute-start | bytes 1769480 | tf_op jit(solution)/shard_map/ppermute | solution.py:49
  69.7 5.1 %collective-permute-start.21 = (bf16[8,144,256]{2,1,0:T(8,128)(2,1)S(1)}, bf16[8,144,256]{2,1,0:T(8,128)(2,1)S(1)}, u32[]{:S(2)}, u32[]{:S(2)}) collective-permute-start(bf16[8,144,256]{2,1,0:T(8,128)(2,1)S(1)} %copy-done.6), channel_id=1, source_target_pairs={{1,0},{0,1},{5,4},{4,5},{9,8},{8,9},{13,12},{12,13},{33,32},{32,33... | collective-permute-start | bytes 1769480 | tf_op jit(solution)/shard_map/ppermute | solution.py:49
  70.0 4.8 %collective-permute-start.22 = (bf16[8,144,256]{2,1,0:T(8,128)(2,1)S(1)}, bf16[8,144,256]{2,1,0:T(8,128)(2,1)S(1)}, u32[]{:S(2)}, u32[]{:S(2)}) collective-permute-start(bf16[8,144,256]{2,1,0:T(8,128)(2,1)S(1)} %copy-done.4), channel_id=1, source_target_pairs={{1,0},{0,1},{5,4},{4,5},{9,8},{8,9},{13,12},{12,13},{33,32},{32,33... | collective-permute-start | bytes 1769480 | tf_op jit(solution)/shard_map/ppermute | solution.py:49
  71.0 3.1 %collective-permute-start.17 = (bf16[8,128,256]{2,1,0:T(8,128)(2,1)S(1)}, bf16[8,128,256]{2,1,0:T(8,128)(2,1)S(1)}, u32[]{:S(2)}, u32[]{:S(2)}) collective-permute-start(bf16[8,128,256]{2,1,0:T(8,128)(2,1)S(1)} %copy-done.12), channel_id=1, source_target_pairs={{1,0},{0,1},{5,4},{4,5},{9,8},{8,9},{13,12},{12,13},{33,32},{32,33... | collective-permute-start | bytes 1572872 | tf_op jit(solution)/shard_map/ppermute | solution.py:49
  71.2 3.6 %collective-permute-start.18 = (bf16[8,128,256]{2,1,0:T(8,128)(2,1)S(1)}, bf16[8,128,256]{2,1,0:T(8,128)(2,1)S(1)}, u32[]{:S(2)}, u32[]{:S(2)}) collective-permute-start(bf16[8,128,256]{2,1,0:T(8,128)(2,1)S(1)} %copy-done.10), channel_id=1, source_target_pairs={{1,0},{0,1},{5,4},{4,5},{9,8},{8,9},{13,12},{12,13},{33,32},{32,33... | collective-permute-start | bytes 1572872 | tf_op jit(solution)/shard_map/ppermute | solution.py:49
  113.9 8.5 %copy-start = (f32[256,256]{1,0:T(8,128)S(1)}, f32[256,256]{1,0:T(8,128)}, u32[]{:S(2)}) copy-start(f32[256,256]{1,0:T(8,128)} %get-tuple-element.32) | copy-start | bytes 786436
  113.9 12.7 %copy-start.24 = (bf16[512]{0:T(512)(128)(2,1)S(1)}, bf16[512]{0:T(512)(128)(2,1)}, u32[]{:S(2)}) copy-start(bf16[512]{0:T(512)(128)(2,1)} %param.7) | copy-start | bytes 3076
  113.9 113.4 %all-to-all-start = ((bf16[128,128,256]{2,1,0:T(8,128)(2,1)}), bf16[128,128,256]{2,1,0:T(8,128)(2,1)}, u32[]{:S(2)}, u32[]{:S(2)}) async-start(bf16[128,128,256]{2,1,0:T(8,128)(2,1)} %get-tuple-element.33), calls=%async_computation | async-start | bytes 16777216 | tf_op jit(solution)/shard_map/all_to_all | solution.py:436
  122.5 1.4 collective-permute-start.23
  123.9 95.8 %collective-permute-start.26 = (f32[128,256]{1,0:T(8,128)S(1)}, f32[128,256]{1,0:T(8,128)S(1)}, u32[]{:S(2)}, u32[]{:S(2)}) collective-permute-start(f32[128,256]{1,0:T(8,128)S(1)} %select_add_fusion), channel_id=1, source_target_pairs={{18,0},{19,1},{22,4},{23,5},{26,8},{27,9},{30,12},{31,13},{50,32},... | collective-permute-start | bytes 393224 | tf_op jit(solution)/shard_map/ppermute | solution.py:49
  124.3 95.4 %collective-permute-start.25 = (f32[128,256]{1,0:T(8,128)S(1)}, f32[128,256]{1,0:T(8,128)S(1)}, u32[]{:S(2)}, u32[]{:S(2)}) collective-permute-start(f32[128,256]{1,0:T(8,128)S(1)} %select_add_fusion), channel_id=1, source_target_pairs={{16,0},{17,1},{20,4},{21,5},{24,8},{25,9},{28,12},{29,13},{48,32},... | collective-permute-start | bytes 393224 | tf_op jit(solution)/shard_map/ppermute | solution.py:49
  125.5 96.4 %collective-permute-start.24 = (f32[128,256]{1,0:T(8,128)S(1)}, f32[128,256]{1,0:T(8,128)S(1)}, u32[]{:S(2)}, u32[]{:S(2)}) collective-permute-start(f32[128,256]{1,0:T(8,128)S(1)} %select_add_fusion), channel_id=1, source_target_pairs={{2,0},{3,1},{6,4},{7,5},{10,8},{11,9},{14,12},{15,13},{34,32},{35,... | collective-permute-start | bytes 393224 | tf_op jit(solution)/shard_map/ppermute | solution.py:49
  227.3 16.3 %collective-permute-start.29 = (f32[128,256]{1,0:T(8,128)S(1)}, f32[128,256]{1,0:T(8,128)S(1)}, u32[]{:S(2)}, u32[]{:S(2)}) collective-permute-start(f32[128,256]{1,0:T(8,128)S(1)} %add_add_fusion.2), channel_id=1, source_target_pairs={{96,0},{97,1},{100,4},{101,5},{104,8},{105,9},{108,12},{109,13},{0... | collective-permute-start | bytes 393224 | tf_op jit(solution)/shard_map/ppermute | solution.py:49
  227.3 16.3 %collective-permute-start.28 = (f32[128,256]{1,0:T(8,128)S(1)}, f32[128,256]{1,0:T(8,128)S(1)}, u32[]{:S(2)}, u32[]{:S(2)}) collective-permute-start(f32[128,256]{1,0:T(8,128)S(1)} %add_add_fusion.2), channel_id=1, source_target_pairs={{32,0},{33,1},{36,4},{37,5},{40,8},{41,9},{44,12},{45,13},{64,32},... | collective-permute-start | bytes 393224 | tf_op jit(solution)/shard_map/ppermute | solution.py:49
  231.4 12.3 %collective-permute-start.27 = (f32[128,256]{1,0:T(8,128)S(1)}, f32[128,256]{1,0:T(8,128)S(1)}, u32[]{:S(2)}, u32[]{:S(2)}) collective-permute-start(f32[128,256]{1,0:T(8,128)S(1)} %add_add_fusion.2), channel_id=1, source_target_pairs={{64,0},{65,1},{68,4},{69,5},{72,8},{73,9},{76,12},{77,13},{96,32},... | collective-permute-start | bytes 393224 | tf_op jit(solution)/shard_map/ppermute | solution.py:49
  243.7 7.0 %collective-permute-start.32 = (f32[128,256]{1,0:T(8,128)S(1)}, f32[128,256]{1,0:T(8,128)S(1)}, u32[]{:S(2)}, u32[]{:S(2)}) collective-permute-start(f32[128,256]{1,0:T(8,128)S(1)} %add_add_fusion.1), channel_id=1, source_target_pairs={{12,0},{13,1},{0,4},{1,5},{4,8},{5,9},{8,12},{9,13},{44,32},{45,33... | collective-permute-start | bytes 393224 | tf_op jit(solution)/shard_map/ppermute | solution.py:49
  243.8 7.0 %collective-permute-start.31 = (f32[128,256]{1,0:T(8,128)S(1)}, f32[128,256]{1,0:T(8,128)S(1)}, u32[]{:S(2)}, u32[]{:S(2)}) collective-permute-start(f32[128,256]{1,0:T(8,128)S(1)} %add_add_fusion.1), channel_id=1, source_target_pairs={{4,0},{5,1},{8,4},{9,5},{12,8},{13,9},{0,12},{1,13},{36,32},{37,33... | collective-permute-start | bytes 393224 | tf_op jit(solution)/shard_map/ppermute | solution.py:49
  247.9 7.3 %collective-permute-start.30 = (f32[128,256]{1,0:T(8,128)S(1)}, f32[128,256]{1,0:T(8,128)S(1)}, u32[]{:S(2)}, u32[]{:S(2)}) collective-permute-start(f32[128,256]{1,0:T(8,128)S(1)} %add_add_fusion.1), channel_id=1, source_target_pairs={{8,0},{9,1},{12,4},{13,5},{0,8},{1,9},{4,12},{5,13},{40,32},{41,33... | collective-permute-start | bytes 393224 | tf_op jit(solution)/shard_map/ppermute | solution.py:49
  255.2 2.4 collective-permute-start.33
  (13 other events, 33.3 us)
